TPU v7x, 512 devices: a whole 4x4x16 slice. The times are simulated.
512 devices in a mesh: prompt: 16 (over z), seq: 32 (over y, x, core).
Axes of the slice: x: 4, y: 4, z: 16, core: 2. Of those that a mesh axis runs over, the one named last changes fastest.
Arguments:
- queries: bfloat16 [16, 32, 2, 32, 128], P('prompt', 'seq'), may hold values from -160 to 160
- prompt_key_cache: bfloat16 [16, 4, 8192, 128], P('prompt', None, 'seq'), may hold values from -5 to 5
- prompt_value_cache: bfloat16 [16, 4, 8192, 128], P('prompt', None, 'seq'), may hold values from -6 to 6
- kept: int32 [16, 4, 32], P('prompt', None, 'seq'), may hold values from 1 to 2, as said below
- sample_keys: bfloat16 [16, 32, 4, 256, 128], P('prompt', 'seq'), may hold values from -6 to 6
- sample_values: bfloat16 [16, 32, 4, 256, 128], P('prompt', 'seq'), may hold values from -6 to 6
- suffix_len: int32 [16, 32], P('prompt', 'seq'), may hold values from 1 to 256, as said below
- decode_keys: bfloat16 [16, 32, 2, 4, 128], P('prompt', 'seq'), may hold values from -6 to 6
- decode_values: bfloat16 [16, 32, 2, 4, 128], P('prompt', 'seq'), may hold values from -6 to 6
- out_weight: bfloat16 [4096, 8192], P('seq', 'prompt'), may hold values from -0.1875 to 0.1875
Outputs:
- attn_out: bfloat16 [1024, 8192], P('seq', 'prompt')
Inputs may be any that keep to these rules, and one draw needn't show every extreme that they name: `kept`: for every prompt and key-value head some seq index has all 2 slots live. `suffix_len`: in every prompt some sample has 256 generated tokens.
All inputs are finite; a program needn't handle non-finite values.
Results may differ from a plain program's by a relative error of at most 0.0048.
Values may be sent and summed in bfloat16 or wider, within the bound.
A program may use at most 128 MiB of HBM per device.

v0:
```python
import math

import jax
import jax.numpy as jnp
from jax import lax
from jax.sharding import PartitionSpec as P

BLOCK_TOKENS = 128
KEPT_SLOTS = 2


NEGATIVE = -1e30


def joined(x, axis, combine):
    everything = jax.tree.map(lambda part: lax.all_gather(part, axis), x)
    initial = jax.tree.map(lambda part: part[0], everything)

    def lap(k, so_far):
        return combine(so_far, jax.tree.map(lambda part: part[k], everything))

    return lax.fori_loop(1, lax.axis_size(axis), lap, initial)


def combine(earlier, later):
    highest = jnp.maximum(earlier[0], later[0])
    early_factor = jnp.exp(earlier[0] - highest)
    late_factor = jnp.exp(later[0] - highest)
    softmax_total = earlier[1] * early_factor + later[1] * late_factor
    summed = earlier[2] * early_factor[..., None] + later[2] * late_factor[..., None]
    return (highest, softmax_total, summed)


def on_device(
    queries,
    prompt_key_cache,
    prompt_value_cache,
    kept,
    sample_keys,
    sample_values,
    suffix_len,
    decode_keys,
    decode_values,
    out_weight,
):
    seq_count = lax.axis_size("seq")
    seq_index = lax.axis_index("seq")
    own_count = queries.shape[1]
    step_count = queries.shape[2]
    head_count = queries.shape[3]
    head_dim = queries.shape[4]
    kv_count = prompt_key_cache.shape[1]
    group_size = head_count // kv_count
    logit_scale = 1.0 / math.sqrt(head_dim)
    gathered = lax.all_gather(queries, "seq", axis=1, tiled=True)
    sample_count = gathered.shape[1]
    grouped_queries = gathered[0].reshape(sample_count, step_count, kv_count, group_size, head_dim)
    query_rows = jnp.transpose(grouped_queries, (2, 0, 1, 3, 4)).reshape(
        kv_count, sample_count * step_count * group_size, head_dim
    )
    key_cache_store = prompt_key_cache[0].reshape(kv_count, KEPT_SLOTS, BLOCK_TOKENS, head_dim)
    value_cache_store = prompt_value_cache[0].reshape(kv_count, KEPT_SLOTS, BLOCK_TOKENS, head_dim)
    kept_block_counts = kept[0, :, 0]
    active_mask = jnp.arange(KEPT_SLOTS, dtype=jnp.int32)[None, :] < kept_block_counts[:, None]

    def one_head(pieces):
        head_row_block, key_block_list, value_block_list, live_blocks = pieces
        logit_scores = (
            jnp.einsum(
                "eg,mxg->emx", head_row_block, key_block_list, preferred_element_type=jnp.float32
            )
            * logit_scale
        )
        block_max = jnp.where(live_blocks[None, :], jnp.max(logit_scores, axis=2), NEGATIVE)
        attention_weights = jnp.where(
            live_blocks[None, :, None], jnp.exp(logit_scores - block_max[:, :, None]), 0.0
        )
        block_sum = jnp.sum(attention_weights, axis=2)
        block_output = jnp.einsum(
            "yaf,afi->yai",
            attention_weights.astype(jnp.bfloat16),
            value_block_list,
            preferred_element_type=jnp.float32,
        )
        highest = jnp.max(block_max, axis=1)
        factor = jnp.exp(block_max - highest[:, None])
        return (
            highest,
            jnp.sum(factor * block_sum, axis=1),
            jnp.sum(factor[:, :, None] * block_output, axis=1),
        )

    prompt_maximum, prompt_sum, prompt_output = lax.map(
        one_head, (query_rows, key_cache_store, value_cache_store, active_mask)
    )
    own_queries = queries[0].reshape(own_count, step_count, kv_count, group_size, head_dim)
    suffix_scores = (
        jnp.einsum(
            "nthgd,nhid->nhtgi", own_queries, sample_keys[0], preferred_element_type=jnp.float32
        )
        * logit_scale
    )
    fresh_scores = (
        jnp.einsum(
            "nthgd,nuhd->nhtgu", own_queries, decode_keys[0], preferred_element_type=jnp.float32
        )
        * logit_scale
    )
    position = jnp.arange(sample_keys.shape[3], dtype=jnp.int32)
    sample_token_mask = (position[None, :] < suffix_len[0][:, None])[:, None, None, None, :]
    step_index = jnp.arange(step_count, dtype=jnp.int32)
    newest_token_mask = (step_index[None, :] <= step_index[:, None])[None, None, :, None, :]
    tail_max = jnp.maximum(
        jnp.max(jnp.where(sample_token_mask, suffix_scores, NEGATIVE), axis=4),
        jnp.max(jnp.where(newest_token_mask, fresh_scores, NEGATIVE), axis=4),
    )
    suffix_weights = jnp.where(sample_token_mask, jnp.exp(suffix_scores - tail_max[..., None]), 0.0)
    fresh_weights = jnp.where(newest_token_mask, jnp.exp(fresh_scores - tail_max[..., None]), 0.0)
    tail_sum = jnp.sum(suffix_weights, axis=4) + jnp.sum(fresh_weights, axis=4)
    tail_out = jnp.einsum(
        "nhtgi,nhid->nhtgd",
        suffix_weights.astype(jnp.bfloat16),
        sample_values[0],
        preferred_element_type=jnp.float32,
    )
    tail_out = tail_out + jnp.einsum(
        "nhtgu,nuhd->nhtgd",
        fresh_weights.astype(jnp.bfloat16),
        decode_values[0],
        preferred_element_type=jnp.float32,
    )
    tail_part = (
        jnp.transpose(tail_max, (1, 0, 2, 3)),
        jnp.transpose(tail_sum, (1, 0, 2, 3)),
        jnp.transpose(tail_out, (1, 0, 2, 3, 4)),
    )
    prefix = (
        prompt_maximum.reshape(kv_count, sample_count, step_count, group_size),
        prompt_sum.reshape(kv_count, sample_count, step_count, group_size),
        prompt_output.reshape(kv_count, sample_count, step_count, group_size, head_dim),
    )
    offset = seq_index * own_count
    own_part = tuple((lax.dynamic_slice_in_dim(member, offset, own_count, 1) for member in prefix))
    merged = combine(own_part, tail_part)
    prefix = tuple(
        (
            lax.dynamic_update_slice_in_dim(member, update, offset, 1)
            for member, update in zip(prefix, merged)
        )
    )
    part_max = jnp.transpose(prefix[0], (1, 2, 0, 3)).reshape(sample_count, step_count, head_count)
    part_total = jnp.transpose(prefix[1], (1, 2, 0, 3)).reshape(
        sample_count, step_count, head_count
    )
    part_out = jnp.transpose(prefix[2], (1, 2, 0, 3, 4)).reshape(
        sample_count, step_count, head_count, head_dim
    )
    local_heads = head_count // seq_count
    highest, softmax_total, summed = joined((part_max, part_total, part_out), "seq", combine)
    highest = lax.dynamic_slice_in_dim(highest, seq_index * local_heads, local_heads, 2)
    softmax_total = lax.dynamic_slice_in_dim(softmax_total, seq_index * local_heads, local_heads, 2)
    summed = lax.dynamic_slice_in_dim(summed, seq_index * local_heads, local_heads, 2)
    head_out = (
        (summed / softmax_total[..., None])
        .astype(jnp.bfloat16)
        .reshape(sample_count * step_count, local_heads * head_dim)
    )
    all_rows = lax.all_gather(head_out, "prompt", axis=0, tiled=True)
    result = lax.psum_scatter(
        jnp.dot(all_rows, out_weight, preferred_element_type=jnp.float32),
        "seq",
        scatter_dimension=0,
        tiled=True,
    )
    return result.astype(jnp.bfloat16)


def solution(mesh):
    placed = (
        P("prompt", "seq", None, None, None),
        P("prompt", None, "seq", None),
        P("prompt", None, "seq", None),
        P("prompt", None, "seq"),
        P("prompt", "seq", None, None, None),
        P("prompt", "seq", None, None, None),
        P("prompt", "seq"),
        P("prompt", "seq", None, None, None),
        P("prompt", "seq", None, None, None),
        P("seq", "prompt"),
    )
    return jax.shard_map(
        on_device, mesh=mesh, in_specs=placed, out_specs=P("seq", "prompt"), check_vma=False
    )
```

profile of v0, /device:TPU:1, one launch (start us, length us, event | category | flops | bytes accessed | tf_op | source)
XLA Modules:
  0.0 388.1 jit_solution(14444092180296759480)
XLA Ops:
  7.3 0.7 iota_compare_fusion
  8.0 29.2 %all_gather.15 = bf16[1,32,2,32,128]{4,3,2,0,1:T(8,128)(2,1)S(1)} all-gather(bf16[1,1,2,32,128]{4,3,2,0,1:T(8,128)(2,1)} %bitcast.184), channel_id=1, replica_groups=mesh['prompt'=16,'seq'=32] {'seq'}, dimensions={1}, use_global_device_ids=true | all-gather | bytes 540672 | tf_op jit(solution)/shard_map/all_gather | solution.py:55
  37.3 11.2 %while.33 = (s32[]{:T(128)}, f32[4,512]{1,0:T(4,128)S(1)}, f32[4,512]{1,0:T(4,128)S(1)}, f32[4,512,128]{2,1,0:T(8,128)S(1)}, pred[4,2]{1,0:T(4,128)(4,1)S(1)}, /...) while((s32[]{:T(128)}, f32[4,512]{1,0:T(4,128)S(1)}, ...), condition=%wide.region_6.7_spmd, body=%wide.region_0.6_spmd.sunk | while | flops 68356096 | bytes 3202187 | solution.py:93
  37.3 1.1 fusion.67
  38.5 0.1 fusion.69
  38.6 1.2 fusion.70
  40.1 1.1 fusion.67
  41.3 0.1 fusion.69
  41.4 1.2 fusion.70
  42.9 1.1 fusion.67
  44.1 0.1 fusion.69
  44.2 1.2 fusion.70
  45.7 1.1 fusion.67
  46.9 0.1 fusion.69
  47.0 1.2 fusion.70
  48.5 0.2 reshape.198
  48.7 0.9 select_reduce_fusion.1
  49.7 1.0 select_reduce_fusion
  50.8 0.2 fusion.30
  51.0 1.2 fusion.26
  52.1 0.2 reshape.202
  52.4 0.9 fusion.25
  53.3 1.1 copy_bitcast_fusion.2
  54.9 25.0 %all_gather.16 = f32[32,32,2,32]{3,1,2,0:T(8,128)S(1)} all-gather(f32[1,32,2,32]{3,1,2,0:T(8,128)S(1)} %copy.49), channel_id=1, replica_groups=mesh['prompt'=16,'seq'=32] {'seq'}, dimensions={0}, use_global_device_ids=true | all-gather | bytes 270336 | tf_op jit(solution)/shard_map/all_gather | solution.py:16
  79.9 22.9 %all_gather.17 = f32[32,32,2,32]{3,1,2,0:T(8,128)S(1)} all-gather(f32[1,32,2,32]{3,1,2,0:T(8,128)S(1)} %copy.53), channel_id=1, replica_groups=mesh['prompt'=16,'seq'=32] {'seq'}, dimensions={0}, use_global_device_ids=true | all-gather | bytes 270336 | tf_op jit(solution)/shard_map/all_gather | solution.py:16
  102.9 81.6 %all-gather.2.cloned.1.call-done = f32[32,32,2,32,128]{4,3,2,1,0:T(8,128)} async-done(((f32[1,32,2,32,128]{4,3,2,1,0:T(8,128)}), f32[32,32,2,32,128]{4,3,2,1,0:T(8,128)}) %all-gather.2.cloned.1.call-update) | async-done | bytes 33554448 | tf_op jit(solution)/shard_map/all_gather | solution.py:16
  184.5 1.3 slice_bitcast_fusion
  185.8 63.3 %while.34 = (s32[]{:T(128)}, f32[32,2,32]{2,1,0:T(2,128)S(1)}, f32[32,2,32]{2,1,0:T(2,128)S(1)}, f32[32,2,32,128]{3,2,1,0:T(8,128)S(1)}, f32[32,32,2,32]{3,1,2,0...) while((s32[]{:T(128)}, f32[32,2,32]{2,1,0:T(2,128)S(1)}, ...), condition=%wide.region_12.13_spmd, body=%wide.region_11.12_spmd.sunk | while | flops 798725 | bytes 3260559 | solution.py:22
  186.0 1.9 fusion.72
  188.0 1.9 fusion.72
  190.1 1.9 fusion.72
  192.1 1.9 fusion.72
  194.1 1.9 fusion.72
  196.2 1.9 fusion.72
  198.2 1.9 fusion.72
  200.3 1.9 fusion.72
  202.3 1.9 fusion.72
  204.3 1.9 fusion.72
  206.4 1.9 fusion.72
  208.4 1.9 fusion.72
  210.5 1.9 fusion.72
  212.5 1.9 fusion.72
  214.6 1.9 fusion.72
  216.6 1.9 fusion.72
  218.6 1.9 fusion.72
  220.7 1.9 fusion.72
  222.7 1.9 fusion.72
  224.8 1.9 fusion.72
  226.8 1.9 fusion.72
  228.8 1.9 fusion.72
  230.9 1.9 fusion.72
  232.9 1.9 fusion.72
  235.0 1.9 fusion.72
  237.0 1.9 fusion.72
  239.1 1.9 fusion.72
  241.1 1.9 fusion.72
  243.1 1.9 fusion.72
  245.2 1.9 fusion.72
  247.2 1.9 fusion.72
  249.4 0.1 divide_convert_fusion
  249.6 25.0 %all_gather.19 = bf16[1024,128]{1,0:T(8,128)(2,1)S(1)} all-gather(bf16[64,128]{1,0:T(8,128)(2,1)S(1)} %bitcast.185), channel_id=1, replica_groups=mesh['prompt'=16,'seq'=32] {'prompt'}, dimensions={0}, use_global_device_ids=true | all-gather | bytes 278528 | tf_op jit(solution)/shard_map/all_gather | solution.py:168
  274.6 2.7 fusion.51
  277.3 102.5 %reduce-scatter.2.cloned.1.call-done = f32[32,512]{1,0:T(8,128)} async-done(((f32[1024,512]{1,0:T(8,128)}), f32[32,512]{1,0:T(8,128)}) %reduce-scatter.2.cloned.1.call-update) | async-done | bytes 65552 | tf_op jit(solution)/shard_map/reduce_scatter | solution.py:169
  379.8 1.5 convert_element_type.20
  (118 shorter events, 6.2 us)
Async XLA Ops:
  6.5 43.1 %copy-start = (bf16[1,1,4,256,128]{4,3,2,1,0:T(8,128)(2,1)S(1)}, bf16[1,1,4,256,128]{4,3,2,1,0:T(8,128)(2,1)}, u32[]{:S(2)}) copy-start(bf16[1,1,4,256,128]{4,3,2,1,0:T(8,128)(2,1)} %param.18) | copy-start | bytes 786436
  6.5 178.0 %all-gather.2.cloned.1.call-start = ((), (), s32[]{:S(2)}) async-start(), calls=%async_computation.1 | async-start | bytes 34603008 | tf_op jit(solution)/shard_map/all_gather | solution.py:16
  54.5 325.3 %reduce-scatter.2.cloned.1.call-start = ((), (), s32[]{:S(2)}) async-start(), calls=%async_computation.2 | async-start | bytes 2162688 | tf_op jit(solution)/shard_map/reduce_scatter | solution.py:169
Sparse Core Ops, SparseCore 0:
  54.6 129.8 all-gather.1
  277.4 102.3 reduce-scatter.1
where the time goes:
time: 391 us; the launch traced here: 388 us
  waiting for transfers between devices  184 us (47%)
  blocking collectives  102 us (26%)
  other arithmetic  65.6 us (17%)
  matrix products  15.6 us (4%)
  between operations  14.2 us (4%)
  local copies, waits for them, and re-layouts  5.13 us (1%)
    reduce_scatter x1, waiting for transfers between devices, on_device(): lax.psum_scatter(jnp.dot(all_rows, out_weight, preferred_element_type=jnp...  102 us
    all_gather x1, waiting for transfers between devices, joined(): everything = jax.tree.map(lambda part: lax.all_gather(part, axis), x)  81.6 us
    add x31, other arithmetic, combine(): earlier[2] * early_factor[..., None] + later[2] * late_factor[..., None]  58.6 us
    all_gather x2, blocking collectives, joined(): everything = jax.tree.map(lambda part: lax.all_gather(part, axis), x)  47.9 us
    all_gather x1, blocking collectives, on_device(): gathered = lax.all_gather(queries, 'seq', axis=1, tiled=True)  29.2 us
    all_gather x1, blocking collectives, on_device(): all_rows = lax.all_gather(head_out, 'prompt', axis=0, tiled=True)  25 us
  transfers between devices with their start and end apart: 2, of which 2 were waited for; matrix products, arithmetic and copies ran while one was open for 0% of the time, Pallas kernels for 0%

commit v1 on v0

v1 whole, which is shorter than its diff:
```python
import functools
import math

import jax
import jax.numpy as jnp
from jax import lax
from jax.experimental import pallas as pl
from jax.experimental.pallas import tpu as pltpu
from jax.sharding import PartitionSpec as P

MESH = pl.DeviceIdType.MESH
bf16 = jnp.bfloat16
f32 = jnp.float32
NEGATIVE = -1e30

NP = 16
NS = 32
SCALE = 1.0 / math.sqrt(128)
FAR, NEAR = (6, -6, 3, -3), (1, -1)
HOPS = sorted(
    ((dy, dx) for dy in range(4) for dx in range(4)),
    key=lambda t: -(min(t[0], 4 - t[0]) + min(t[1], 4 - t[1])),
)
NT = (((1,), (1,)), ((), ()))
TN = (((0,), (0,)), ((), ()))


def dot(a, b, dims=(((1,), (0,)), ((), ()))):
    return lax.dot_general(a, b, dims, preferred_element_type=f32)


def iota(shape, axis):
    return lax.broadcasted_iota(jnp.int32, shape, axis)


def kernel(
    q_ref, k_ref, v_ref, kept_ref, sk_ref, sv_ref, len_ref, dk_ref, dv_ref, w_ref,
    out_ref,
    qv, qsend, qbuf, kbuf, vbuf, vt, skv, svv, dkv, dvv, flag_out, flag, qpl,
    tail_out, tail, part, rbuf, zbuf, wbuf, psend, obuf,
    lsem, ssem, rsem, zssem, zrsem,
):
    p, s = lax.axis_index("prompt"), lax.axis_index("seq")
    y, i = lax.div(s, 8), lax.rem(s, 8)
    x, c = lax.div(i, 2), lax.rem(s, 2)
    chip, other = lax.div(s, 2), 1 - c
    sib = s + 1 - 2 * c

    def at(plane, seq):
        return {"prompt": plane, "seq": seq}

    def zoff(o):
        return lax.rem(p + o + NP, NP)

    def remote(src, dst, send, recv, plane, seq):
        return pltpu.make_async_remote_copy(
            src, dst, send, recv, device_id=at(plane, seq), device_id_type=MESH
        )

    def wait_bytes(ref, sem):
        pltpu.make_async_copy(ref, ref, sem).wait()

    def send_or_keep(src, dst, n, seq):
        own = seq == s

        @pl.when(own)
        def _():
            pltpu.make_async_copy(src, dst, rsem.at[n]).start()

        @pl.when(jnp.logical_not(own))
        def _():
            remote(src, dst, ssem.at[n], rsem.at[n], p, seq).start()

    local = [
        pltpu.make_async_copy(q_ref.at[0, 0], qv, lsem.at[0]),
        pltpu.make_async_copy(sk_ref.at[0, 0], skv, lsem.at[1]),
        pltpu.make_async_copy(dk_ref.at[0, 0], dkv, lsem.at[2]),
        pltpu.make_async_copy(sv_ref.at[0, 0], svv, lsem.at[3]),
        pltpu.make_async_copy(dv_ref.at[0, 0], dvv, lsem.at[4]),
        pltpu.make_async_copy(k_ref.at[0, pl.ds(2 * c, 2)], kbuf.at[c], lsem.at[5]),
        pltpu.make_async_copy(v_ref.at[0, pl.ds(2 * c, 2)], vbuf.at[c], lsem.at[6]),
    ]
    for copy in local:
        copy.start()

    barrier = pltpu.get_barrier_semaphore()

    def greet(k, carry):
        pl.semaphore_signal(
            barrier, inc=1, device_id=at(p, lax.rem(s + k, NS)), device_id_type=MESH
        )
        return carry

    lax.fori_loop(1, NS, greet, 0)
    zpartners = (1, -1, 2, -2, 3, -3, 6, -6)
    for o in zpartners:
        pl.semaphore_signal(barrier, inc=1, device_id=at(zoff(o), s), device_id_type=MESH)

    local[0].wait()
    heads = qv[...].astype(f32).reshape(2, 4, 8, 128)
    for h in range(4):
        rows = heads[:, h].reshape(16, 128).astype(bf16)
        qsend[h] = rows
    row8 = iota((8, 128), 0)

    def flags(core):
        first = kept_ref[0, 2 * core, 0].astype(f32)
        second = kept_ref[0, 2 * core + 1, 0].astype(f32)
        return jnp.where(row8 == 0, first, second)

    flag[c] = flags(c)
    flag_out[...] = flags(other)

    pl.semaphore_wait(barrier, NS - 1 + len(zpartners))

    for dy, dx in HOPS:
        base = lax.rem(y + dy, 4) * 8 + lax.rem(x + dx, 4) * 2
        for core in range(2):
            if (dy, dx) != (0, 0):
                remote(
                    qsend.at[pl.ds(2 * core, 2)], qbuf.at[s], ssem.at[0], rsem.at[0], p, base + core
                ).start()
    remote(qsend.at[pl.ds(2 * other, 2)], qbuf.at[s], ssem.at[0], rsem.at[0], p, sib).start()
    pltpu.make_async_copy(qsend.at[pl.ds(2 * c, 2)], qbuf.at[s], rsem.at[0]).start()
    swap = [
        remote(k_ref.at[0, pl.ds(2 * other, 2)], kbuf.at[c], ssem.at[1], rsem.at[1], p, sib),
        remote(v_ref.at[0, pl.ds(2 * other, 2)], vbuf.at[c], ssem.at[2], rsem.at[2], p, sib),
        remote(flag_out, flag.at[c], ssem.at[3], rsem.at[3], p, sib),
    ]
    for copy in swap:
        copy.start()
    for dx in (2, 1, 3, 0):
        for half in range(2):
            send_or_keep(
                w_ref.at[pl.ds(64 * half, 64)], wbuf.at[i], 4, y * 8 + lax.rem(x + dx, 4) * 2 + half
            )

    lane = iota((1, 128), 1)
    qpl[...] = jnp.zeros((4, 128, 128), bf16)
    for h in range(4):
        qpl[h, pl.ds(pl.multiple_of(16 * i, 16), 16), :] = qsend[h]
    for copy in local[1:5]:
        copy.wait()
    placed = qpl[...].reshape(512, 128)
    fresh = [dot(dkv[u], placed, NT) * SCALE for u in range(2)]
    later_step = lax.rem(lax.div(lane, 8), 2) == 1
    key_mask = iota((256, 128), 0) < len_ref[0, 0]
    row16 = iota((16, 128), 0)
    for h in range(4):
        scores = dot(skv[h], qpl[h], NT) * SCALE
        scores = jnp.where(key_mask, scores, NEGATIVE)
        f0 = fresh[0][h : h + 1, 128 * h : 128 * h + 128]
        f1 = jnp.where(later_step, fresh[1][h : h + 1, 128 * h : 128 * h + 128], NEGATIVE)
        top = jnp.maximum(jnp.max(scores, axis=0, keepdims=True), jnp.maximum(f0, f1))
        e = jnp.where(key_mask, jnp.exp(scores - top), 0.0)
        e0, e1 = jnp.exp(f0 - top), jnp.where(later_step, jnp.exp(f1 - top), 0.0)
        total = jnp.sum(e, axis=0, keepdims=True) + e0 + e1
        value0 = dvv[0].astype(f32)[h : h + 1]
        value1 = dvv[1].astype(f32)[h : h + 1]
        values = jnp.where(row16 == 0, value0, jnp.where(row16 == 1, value1, 0.0)).astype(bf16)
        weights = jnp.where(row16 == 0, e0, jnp.where(row16 == 1, e1, 0.0)).astype(bf16)
        o = dot(svv[h], e.astype(bf16), TN) + dot(values, weights, TN)
        stats = jnp.where(row8 == 0, top, total)
        core, j = h // 2, h % 2

        @pl.when(c == core)
        def _():
            tail[c, j, :128] = o
            tail[c, j, 128:] = stats

        @pl.when(c != core)
        def _():
            tail_out[j, :128] = o
            tail_out[j, 128:] = stats

    tail_copy = remote(tail_out, tail.at[c], ssem.at[5], rsem.at[5], p, sib)
    tail_copy.start()

    local[5].wait()
    local[6].wait()
    for n in (1, 2, 3):
        swap[n - 1].wait_recv()
    for j in range(2):
        for core in range(2):
            vt[j, core] = jnp.transpose(vbuf[core, j])
    tail_copy.wait_recv()

    wait_bytes(qbuf, rsem.at[0])
    for kk in range(4):
        chunk = lax.rem(y + kk, 4)
        for j in range(2):
            rows = qbuf[pl.ds(8 * chunk, 8), j].reshape(128, 128)
            tops, sums, outs = [], [], []
            for core in range(2):
                scores = dot(kbuf[core, j], rows, NT) * SCALE
                for slot in range(2):
                    block = scores[128 * slot : 128 * slot + 128]
                    block_max = jnp.max(block, axis=0, keepdims=True)
                    e = jnp.exp(block - block_max)
                    sums.append(jnp.sum(e, axis=0, keepdims=True))
                    outs.append(dot(vt[j, core, :, 128 * slot : 128 * slot + 128], e.astype(bf16)))
                    if slot == 1:
                        live = flag[core, j : j + 1, :] > 1.5
                        block_max = jnp.where(live, block_max, NEGATIVE)
                    tops.append(block_max)
            if kk == 0:
                for core in range(2):
                    mine = lax.div(lane, 16) == 2 * x + core
                    tops.append(jnp.where(mine, tail[core, j, 128:129], NEGATIVE))
                    sums.append(tail[core, j, 129:130])
                    outs.append(tail[core, j, :128])
            top = functools.reduce(jnp.maximum, tops).astype(bf16).astype(f32)
            total, summed = 0.0, 0.0
            for m, t, o in zip(tops, sums, outs):
                factor = jnp.exp(m - top)
                total = total + factor * t
                summed = summed + factor * o
            high = total.astype(bf16).astype(f32)
            stats = jnp.where(row16 == 0, top, jnp.where(row16 == 1, high, total - high))
            stats = stats.astype(bf16)
            summed = summed.astype(bf16)
            for half in range(2):
                part[kk, j, half, :64] = summed[64 * half : 64 * half + 64]
                part[kk, j, half, 64:] = stats
                send_or_keep(
                    part.at[kk, j, half], rbuf.at[chip], 6, (2 * c + j) * 8 + chunk * 2 + half
                )

    wait_bytes(rbuf, rsem.at[6])
    tops = [rbuf[k, 64:80].astype(f32) for k in range(16)]
    top = functools.reduce(jnp.maximum, [t[0:1] for t in tops])
    total, summed = 0.0, 0.0
    for k in range(16):
        factor = jnp.exp(tops[k][0:1] - top)
        total = total + factor * (tops[k][1:2] + tops[k][2:3])
        summed = summed + factor * rbuf[k, :64].astype(f32)
    head_out = (summed / total).astype(bf16)
    blank = jnp.zeros_like(head_out)
    stacked = jnp.concatenate(
        [jnp.concatenate([head_out, blank], axis=1), jnp.concatenate([blank, head_out], axis=1)],
        axis=0,
    )
    a, b = iota((64, 256), 0), iota((64, 256), 1)
    wanted = lax.rem(a, 16) * 8 + 2 * lax.div(a, 16) + lax.div(b, 128)
    pick = jnp.where(lax.rem(b, 128) == wanted, 1.0, 0.0).astype(bf16)
    laid = dot(pick, stacked, NT).astype(bf16)
    for g in range(4):
        zbuf[p, :, 128 * g : 128 * g + 128] = laid[16 * g : 16 * g + 16]

    sends = []

    def zsend(src, dst, o):
        n = len(sends)
        copy = remote(src, dst, zssem.at[n], zrsem.at[n], zoff(o), s)
        copy.start()
        sends.append(copy)
        return copy

    first = [zsend(zbuf.at[p], zbuf.at[p], o) for o in FAR]
    second = [zsend(zbuf.at[p], zbuf.at[p], o) for o in NEAR]
    for o, copy in zip(FAR, first):
        copy.wait_recv()
        q = zoff(-o)
        if abs(o) == 6:
            lanes = pl.ds(0 if o > 0 else 256, 256)
            part_ref = zbuf.at[q, :, lanes]
            second.append(zsend(part_ref, part_ref, 2 if o > 0 else -2))
        for n in NEAR:
            second.append(zsend(zbuf.at[q], zbuf.at[q], n))
    for copy in second:
        copy.wait_recv()

    wait_bytes(wbuf, rsem.at[4])
    terms = dot(zbuf[...].reshape(256, 512), wbuf[...].reshape(512, 512))
    psend[...] = terms.astype(bf16).reshape(16, 16, 512)
    mine = lax.rem(x, 2) * 8 + 2 * y + c
    for dy, dx in HOPS:
        prompt = lax.rem(y + dy, 4) * 4 + lax.rem(x + dx, 4)
        send_or_keep(psend.at[prompt], obuf.at[mine], 7, 2 * prompt + lax.div(x, 2))
    wait_bytes(obuf, rsem.at[7])
    for half in range(2):
        result = obuf[8 * half].astype(f32)
        for k in range(1, 8):
            result = result + obuf[8 * half + k].astype(f32)
        out_ref[16 * half : 16 * half + 16, :] = result.astype(bf16)

    wait_bytes(qbuf.at[pl.ds(0, 31)], ssem.at[0])
    for copy in swap:
        copy.wait_send()
    tail_copy.wait_send()
    for copy in sends:
        copy.wait_send()
    wait_bytes(wbuf.at[pl.ds(0, 7)], ssem.at[4])
    wait_bytes(rbuf.at[pl.ds(0, 15)], ssem.at[6])
    wait_bytes(obuf.at[pl.ds(0, 15)], ssem.at[7])

    @pl.when(lax.div(y, 2) != c)
    def _():
        wait_bytes(rbuf.at[15], ssem.at[6])

    @pl.when(lax.div(x, 2) != c)
    def _():
        wait_bytes(obuf.at[15], ssem.at[7])


def on_device(*args):
    any_spec = pl.BlockSpec(memory_space=pl.ANY)
    smem = pl.BlockSpec(memory_space=pltpu.SMEM)
    specs = [any_spec] * 10
    specs[3] = specs[6] = smem
    return pl.pallas_call(
        kernel,
        out_shape=jax.ShapeDtypeStruct((32, 512), bf16),
        in_specs=specs,
        out_specs=pl.BlockSpec(memory_space=pltpu.VMEM),
        scratch_shapes=[
            pltpu.VMEM((2, 32, 128), bf16),
            pltpu.VMEM((4, 16, 128), bf16),
            pltpu.VMEM((32, 2, 16, 128), bf16),
            pltpu.VMEM((2, 2, 256, 128), bf16),
            pltpu.VMEM((2, 2, 256, 128), bf16),
            pltpu.VMEM((2, 2, 128, 256), bf16),
            pltpu.VMEM((4, 256, 128), bf16),
            pltpu.VMEM((4, 256, 128), bf16),
            pltpu.VMEM((2, 4, 128), bf16),
            pltpu.VMEM((2, 4, 128), bf16),
            pltpu.VMEM((8, 128), f32),
            pltpu.VMEM((2, 8, 128), f32),
            pltpu.VMEM((4, 128, 128), bf16),
            pltpu.VMEM((2, 136, 128), f32),
            pltpu.VMEM((2, 2, 136, 128), f32),
            pltpu.VMEM((4, 2, 2, 80, 128), bf16),
            pltpu.VMEM((16, 80, 128), bf16),
            pltpu.VMEM((16, 16, 512), bf16),
            pltpu.VMEM((8, 64, 512), bf16),
            pltpu.VMEM((16, 16, 512), bf16),
            pltpu.VMEM((16, 16, 512), bf16),
            pltpu.SemaphoreType.DMA((7,)),
            pltpu.SemaphoreType.DMA((8,)),
            pltpu.SemaphoreType.DMA((8,)),
            pltpu.SemaphoreType.DMA((16,)),
            pltpu.SemaphoreType.DMA((16,)),
        ],
        compiler_params=pltpu.CompilerParams(
            collective_id=0, has_side_effects=True, vmem_limit_bytes=32 * 1024 * 1024
        ),
        name="attend",
    )(*args)


def solution(mesh):
    placed = (
        P("prompt", "seq", None, None, None),
        P("prompt", None, "seq", None),
        P("prompt", None, "seq", None),
        P("prompt", None, "seq"),
        P("prompt", "seq", None, None, None),
        P("prompt", "seq", None, None, None),
        P("prompt", "seq"),
        P("prompt", "seq", None, None, None),
        P("prompt", "seq", None, None, None),
        P("seq", "prompt"),
    )
    return jax.shard_map(
        on_device, mesh=mesh, in_specs=placed, out_specs=P("seq", "prompt"), check_vma=False
    )
```

time: 391 us -> 58.5 us (0.15)
  waiting for transfers between devices: 184 us -> 0 us
  blocking collectives: 102 us -> 0 us
  other arithmetic: 65.6 us -> 0 us
  Pallas kernels: 0 us -> 50.7 us
  matrix products: 15.6 us -> 0 us
  between operations: 14.2 us -> 0.7 us
    reduce_scatter x1 -> x0, waiting for transfers between devices: 102 us -> none  [on_device(): lax.psum_scatter(jnp.dot(all_rows, out_weight, preferred_element_type=jnp...]
    all_gather x4 -> x0, blocking collectives: 102 us -> none  [the longest x2 47.9 us: joined(): everything = jax.tree.map(lambda part: lax.all_gather(part, axis), x)]
    all_gather x1 -> x0, waiting for transfers between devices: 81.6 us -> none  [joined(): everything = jax.tree.map(lambda part: lax.all_gather(part, axis), x)]
    add x62 -> x0, other arithmetic: 61.9 us -> none  [the longest x31 58.6 us: combine(): earlier[2] * early_factor[..., None] + later[2] * late_factor[..., None]]
    pallas_call x0 -> x1, Pallas kernels: none -> 50.7 us  [on_device(): pl.pallas_call(kernel, out_shape=jax.ShapeDtypeStruct((32, 512), bf16), i...]
    dot_general x13 -> x0, matrix products: 15.6 us -> none  [the longest x4 4.64 us: one_head(): jnp.einsum('yaf,afi->yai', attention_weights.astype(jnp.bfloat16), value_...]
    unnamed x3 -> x18, local copies, waits for them, and re-layouts: 0.02 us -> 6.79 us
  transfers between devices with their start and end apart: 2 -> 0, of which waited for: 2 -> 0; matrix products, arithmetic and copies ran while one was open for 0% -> 0% of each run, Pallas kernels for 0% -> 0%
where the time goes in v1:
time: 58.5 us; the launch traced here: 58.1 us
  Pallas kernels  50.7 us (87%)
  local copies, waits for them, and re-layouts  6.79 us (12%)
  between operations  0.7 us (1%)
    pallas_call x1, Pallas kernels, on_device(): pl.pallas_call(kernel, out_shape=jax.ShapeDtypeStruct((32, 512), bf16), i...  50.7 us
    unnamed x18, local copies, waits for them, and re-layouts  6.79 us

profile of v1, /device:TPU:1, one launch (start us, length us, event | category | flops | bytes accessed | tf_op | source)
XLA Modules:
  0.0 58.1 jit_solution(3503498354982230311)
XLA Ops:
  0.0 0.0 copy-start.7
  0.0 0.0 copy-start.6
  0.7 0.7 %copy.11.kept_ref = s32[1,4,1]{2,1,0:T(4,128)S(1)} copy(s32[1,4,1]{1,2,0:T(1,128)} %param.13) | data formatting | bytes 32 | tf_op args[3]
  1.4 0.0 copy-done.7
  1.4 0.0 copy-done.6
  1.4 0.0 copy-start
  1.4 0.9 %copy-done = bf16[1,4,256,128]{3,2,1,0:T(8,128)(2,1)S(1)} copy-done((bf16[1,4,256,128]{3,2,1,0:T(8,128)(2,1)S(1)}, bf16[1,4,256,128]{3,2,1,0:T(8,128)(2,1)}, u32[]{:S(2)}) %copy-start) | copy-done | bytes 262168
  2.4 0.0 copy-start.1
  2.4 0.9 %copy-done.1 = bf16[1,4,256,128]{3,2,1,0:T(8,128)(2,1)S(1)} copy-done((bf16[1,4,256,128]{3,2,1,0:T(8,128)(2,1)S(1)}, bf16[1,4,256,128]{3,2,1,0:T(8,128)(2,1)}, u32[]{:S(2)}) %copy-start.1) | copy-done | bytes 262168
  3.3 0.0 copy-start.2
  3.3 0.9 %copy-done.2 = bf16[1,1,4,256,128]{4,3,2,1,0:T(8,128)(2,1)S(1)} copy-done((bf16[1,1,4,256,128]{4,3,2,1,0:T(8,128)(2,1)S(1)}, bf16[1,1,4,256,128]{4,3,2,1,0:T(8,128)(2,1)}, u32[]{:S(2)}) %copy-start.2) | copy-done | bytes 262168
  4.3 0.0 copy-start.3
  4.3 0.9 %copy-done.3 = bf16[1,1,4,256,128]{4,3,2,1,0:T(8,128)(2,1)S(1)} copy-done((bf16[1,1,4,256,128]{4,3,2,1,0:T(8,128)(2,1)S(1)}, bf16[1,1,4,256,128]{4,3,2,1,0:T(8,128)(2,1)}, u32[]{:S(2)}) %copy-start.3) | copy-done | bytes 262168
  5.2 0.0 copy-start.4
  5.2 0.9 %copy-done.4 = bf16[128,512]{1,0:T(8,128)(2,1)S(1)} copy-done((bf16[128,512]{1,0:T(8,128)(2,1)S(1)}, bf16[128,512]{1,0:T(8,128)(2,1)}, u32[]{:S(2)}) %copy-start.4) | copy-done | bytes 131096
  6.1 0.0 copy-start.5
  6.1 0.7 %copy-done.5 = bf16[1,1,2,32,128]{4,3,2,1,0:T(8,128)(2,1)S(1)} copy-done((bf16[1,1,2,32,128]{4,3,2,1,0:T(8,128)(2,1)S(1)}, bf16[1,1,2,32,128]{4,3,2,1,0:T(8,128)(2,1)}, u32[]{:S(2)}) %copy-start.5) | copy-done | bytes 16408
  6.9 50.7 %attend.1 = bf16[32,512]{1,0:T(8,128)(2,1)S(1)} custom-call(bf16[1,1,2,32,128]{4,3,2,1,0:T(8,128)(2,1)S(1)} %copy-done.5, bf16[1,4,256,128]{3,2,1,0:T(8,128)(2,1)S(1)} %copy-done, bf16[1,4,256,128]{3,2,1,0:T(8,128)(2,1)S(1)} %copy-done.1, s32[1,4,1]{2,1,0:T(4,128)S(1)} %copy.11.kept_ref, bf16[1,1,4,256,128]{4,3,2,1,0:T(8,128)(2,1)S(1)} %copy-done.2, ...), custom_call_target="tpu_custom_call" | custom-call | tf_op jit(solution)/shard_map/attend/pallas_call | solution.py:311
  57.5 0.6 %copy.14 = bf16[32,512]{1,0:T(8,128)(2,1)} copy(bf16[32,512]{1,0:T(8,128)(2,1)S(1)} %attend.1) | data formatting | bytes 65536
Async XLA Ops:
  0.0 1.4 %copy-start.7 = (bf16[1,1,2,4,128]{4,3,2,1,0:T(4,128)(2,1)S(1)}, bf16[1,1,2,4,128]{4,3,2,1,0:T(4,128)(2,1)}, u32[]{:S(2)}) copy-start(bf16[1,1,2,4,128]{4,3,2,1,0:T(4,128)(2,1)} %dv_ref.1) | copy-start | bytes 6148
  0.0 1.4 %copy-start.6 = (bf16[1,1,2,4,128]{4,3,2,1,0:T(4,128)(2,1)S(1)}, bf16[1,1,2,4,128]{4,3,2,1,0:T(4,128)(2,1)}, u32[]{:S(2)}) copy-start(bf16[1,1,2,4,128]{4,3,2,1,0:T(4,128)(2,1)} %dk_ref.1) | copy-start | bytes 6148
  1.4 1.0 %copy-start = (bf16[1,4,256,128]{3,2,1,0:T(8,128)(2,1)S(1)}, bf16[1,4,256,128]{3,2,1,0:T(8,128)(2,1)}, u32[]{:S(2)}) copy-start(bf16[1,4,256,128]{3,2,1,0:T(8,128)(2,1)} %k_ref.1) | copy-start | bytes 786436
  2.4 0.9 %copy-start.1 = (bf16[1,4,256,128]{3,2,1,0:T(8,128)(2,1)S(1)}, bf16[1,4,256,128]{3,2,1,0:T(8,128)(2,1)}, u32[]{:S(2)}) copy-start(bf16[1,4,256,128]{3,2,1,0:T(8,128)(2,1)} %v_ref.1) | copy-start | bytes 786436
  3.3 0.9 %copy-start.2 = (bf16[1,1,4,256,128]{4,3,2,1,0:T(8,128)(2,1)S(1)}, bf16[1,1,4,256,128]{4,3,2,1,0:T(8,128)(2,1)}, u32[]{:S(2)}) copy-start(bf16[1,1,4,256,128]{4,3,2,1,0:T(8,128)(2,1)} %sk_ref.1) | copy-start | bytes 786436
  4.3 0.9 %copy-start.3 = (bf16[1,1,4,256,128]{4,3,2,1,0:T(8,128)(2,1)S(1)}, bf16[1,1,4,256,128]{4,3,2,1,0:T(8,128)(2,1)}, u32[]{:S(2)}) copy-start(bf16[1,1,4,256,128]{4,3,2,1,0:T(8,128)(2,1)} %sv_ref.1) | copy-start | bytes 786436
  5.2 0.9 %copy-start.4 = (bf16[128,512]{1,0:T(8,128)(2,1)S(1)}, bf16[128,512]{1,0:T(8,128)(2,1)}, u32[]{:S(2)}) copy-start(bf16[128,512]{1,0:T(8,128)(2,1)} %w_ref.1) | copy-start | bytes 393220
  6.1 0.7 %copy-start.5 = (bf16[1,1,2,32,128]{4,3,2,1,0:T(8,128)(2,1)S(1)}, bf16[1,1,2,32,128]{4,3,2,1,0:T(8,128)(2,1)}, u32[]{:S(2)}) copy-start(bf16[1,1,2,32,128]{4,3,2,1,0:T(8,128)(2,1)} %q_ref.1) | copy-start | bytes 49156

commit v2 on v1

--- a/solution.py
+++ b/solution.py
@@ -16,7 +16,7 @@
 NP = 16
 NS = 32
 SCALE = 1.0 / math.sqrt(128)
-FAR, NEAR = (6, -6, 3, -3), (1, -1)
+DIRECT = (8, 5, -5, 2, -2, 1, -1)
 HOPS = sorted(
     ((dy, dx) for dy in range(4) for dx in range(4)),
     key=lambda t: -(min(t[0], 4 - t[0]) + min(t[1], 4 - t[1])),
@@ -34,11 +34,11 @@
 
 
 def kernel(
-    q_ref, k_ref, v_ref, kept_ref, sk_ref, sv_ref, len_ref, dk_ref, dv_ref, w_ref,
+    q_ref, k_ref, v_ref, kept_hbm, sk_ref, sv_ref, len_hbm, dk_ref, dv_ref, w_ref,
     out_ref,
     qv, qsend, qbuf, kbuf, vbuf, vt, skv, svv, dkv, dvv, flag_out, flag, qpl,
-    tail_out, tail, part, rbuf, zbuf, wbuf, psend, obuf,
-    lsem, ssem, rsem, zssem, zrsem,
+    tail_out, tail, part, rbuf, laid_ref, zbuf, wbuf, psend, obuf,
+    kept_ref, len_ref, lsem, ssem, rsem, zssem, zrsem,
 ):
     p, s = lax.axis_index("prompt"), lax.axis_index("seq")
     y, i = lax.div(s, 8), lax.rem(s, 8)
@@ -79,6 +79,8 @@
         pltpu.make_async_copy(dv_ref.at[0, 0], dvv, lsem.at[4]),
         pltpu.make_async_copy(k_ref.at[0, pl.ds(2 * c, 2)], kbuf.at[c], lsem.at[5]),
         pltpu.make_async_copy(v_ref.at[0, pl.ds(2 * c, 2)], vbuf.at[c], lsem.at[6]),
+        pltpu.make_async_copy(kept_hbm, kept_ref, lsem.at[7]),
+        pltpu.make_async_copy(len_hbm, len_ref, lsem.at[8]),
     ]
     for copy in local:
         copy.start()
@@ -92,9 +94,9 @@
         return carry
 
     lax.fori_loop(1, NS, greet, 0)
-    zpartners = (1, -1, 2, -2, 3, -3, 6, -6)
-    for o in zpartners:
-        pl.semaphore_signal(barrier, inc=1, device_id=at(zoff(o), s), device_id_type=MESH)
+    for o in DIRECT:
+        for seq in (s, sib):
+            pl.semaphore_signal(barrier, inc=1, device_id=at(zoff(o), seq), device_id_type=MESH)
 
     local[0].wait()
     heads = qv[...].astype(f32).reshape(2, 4, 8, 128)
@@ -104,14 +106,15 @@
     row8 = iota((8, 128), 0)
 
     def flags(core):
-        first = kept_ref[0, 2 * core, 0].astype(f32)
-        second = kept_ref[0, 2 * core + 1, 0].astype(f32)
+        first = kept_ref[0, 0, 2 * core].astype(f32)
+        second = kept_ref[0, 0, 2 * core + 1].astype(f32)
         return jnp.where(row8 == 0, first, second)
 
+    local[7].wait()
     flag[c] = flags(c)
     flag_out[...] = flags(other)
 
-    pl.semaphore_wait(barrier, NS - 1 + len(zpartners))
+    pl.semaphore_wait(barrier, NS - 1 + 2 * len(DIRECT))
 
     for dy, dx in HOPS:
         base = lax.rem(y + dy, 4) * 8 + lax.rem(x + dx, 4) * 2
@@ -129,17 +132,17 @@
     ]
     for copy in swap:
         copy.start()
-    for dx in (2, 1, 3, 0):
-        for half in range(2):
-            send_or_keep(
-                w_ref.at[pl.ds(64 * half, 64)], wbuf.at[i], 4, y * 8 + lax.rem(x + dx, 4) * 2 + half
-            )
+    for dx in (2, 1, 3):
+        remote(
+            w_ref, wbuf.at[c, :, x], ssem.at[4], rsem.at[4], p, y * 8 + lax.rem(x + dx, 4) * 2 + c
+        ).start()
+    pltpu.make_async_copy(w_ref, wbuf.at[c, :, x], rsem.at[4]).start()
 
     lane = iota((1, 128), 1)
     qpl[...] = jnp.zeros((4, 128, 128), bf16)
     for h in range(4):
         qpl[h, pl.ds(pl.multiple_of(16 * i, 16), 16), :] = qsend[h]
-    for copy in local[1:5]:
+    for copy in local[1:5] + local[8:]:
         copy.wait()
     placed = qpl[...].reshape(512, 128)
     fresh = [dot(dkv[u], placed, NT) * SCALE for u in range(2)]
@@ -186,45 +189,53 @@
     tail_copy.wait_recv()
 
     wait_bytes(qbuf, rsem.at[0])
-    for kk in range(4):
+    def partial(kk, j):
         chunk = lax.rem(y + kk, 4)
-        for j in range(2):
-            rows = qbuf[pl.ds(8 * chunk, 8), j].reshape(128, 128)
-            tops, sums, outs = [], [], []
+        rows = qbuf[pl.ds(8 * chunk, 8), j].reshape(128, 128)
+        tops, sums, outs = [], [], []
+        for core in range(2):
+            scores = dot(kbuf[core, j], rows, NT) * SCALE
+            for slot in range(2):
+                block = scores[128 * slot : 128 * slot + 128]
+                block_max = jnp.max(block, axis=0, keepdims=True)
+                e = jnp.exp(block - block_max)
+                sums.append(jnp.sum(e, axis=0, keepdims=True))
+                outs.append(dot(vt[j, core, :, 128 * slot : 128 * slot + 128], e.astype(bf16)))
+                if slot == 1:
+                    live = flag[core, j : j + 1, :] > 1.5
+                    block_max = jnp.where(live, block_max, NEGATIVE)
+                tops.append(block_max)
+        if kk == 0:
             for core in range(2):
-                scores = dot(kbuf[core, j], rows, NT) * SCALE
-                for slot in range(2):
-                    block = scores[128 * slot : 128 * slot + 128]
-                    block_max = jnp.max(block, axis=0, keepdims=True)
-                    e = jnp.exp(block - block_max)
-                    sums.append(jnp.sum(e, axis=0, keepdims=True))
-                    outs.append(dot(vt[j, core, :, 128 * slot : 128 * slot + 128], e.astype(bf16)))
-                    if slot == 1:
-                        live = flag[core, j : j + 1, :] > 1.5
-                        block_max = jnp.where(live, block_max, NEGATIVE)
-                    tops.append(block_max)
-            if kk == 0:
-                for core in range(2):
-                    mine = lax.div(lane, 16) == 2 * x + core
-                    tops.append(jnp.where(mine, tail[core, j, 128:129], NEGATIVE))
-                    sums.append(tail[core, j, 129:130])
-                    outs.append(tail[core, j, :128])
-            top = functools.reduce(jnp.maximum, tops).astype(bf16).astype(f32)
-            total, summed = 0.0, 0.0
-            for m, t, o in zip(tops, sums, outs):
-                factor = jnp.exp(m - top)
-                total = total + factor * t
-                summed = summed + factor * o
-            high = total.astype(bf16).astype(f32)
-            stats = jnp.where(row16 == 0, top, jnp.where(row16 == 1, high, total - high))
-            stats = stats.astype(bf16)
-            summed = summed.astype(bf16)
-            for half in range(2):
-                part[kk, j, half, :64] = summed[64 * half : 64 * half + 64]
-                part[kk, j, half, 64:] = stats
-                send_or_keep(
-                    part.at[kk, j, half], rbuf.at[chip], 6, (2 * c + j) * 8 + chunk * 2 + half
-                )
+                mine = lax.div(lane, 16) == 2 * x + core
+                tops.append(jnp.where(mine, tail[core, j, 128:129], NEGATIVE))
+                sums.append(tail[core, j, 129:130])
+                outs.append(tail[core, j, :128])
+        top = functools.reduce(jnp.maximum, tops).astype(bf16).astype(f32)
+        total, summed = 0.0, 0.0
+        for m, t, o in zip(tops, sums, outs):
+            factor = jnp.exp(m - top)
+            total = total + factor * t
+            summed = summed + factor * o
+        high = total.astype(bf16).astype(f32)
+        stats = jnp.where(row16 == 0, top, jnp.where(row16 == 1, high, total - high))
+        stats = stats.astype(bf16)
+        summed = summed.astype(bf16)
+        for half in range(2):
+            part[kk, j, half, :64] = summed[64 * half : 64 * half + 64]
+            part[kk, j, half, 64:] = stats
+
+    for group in ((0, 1), (2, 3)):
+        for kk in group:
+            for j in range(2):
+                partial(kk, j)
+        for kk in group:
+            chunk = lax.rem(y + kk, 4)
+            for j in range(2):
+                for half in range(2):
+                    send_or_keep(
+                        part.at[kk, j, half], rbuf.at[chip], 6, (2 * c + j) * 8 + chunk * 2 + half
+                    )
 
     wait_bytes(rbuf, rsem.at[6])
     tops = [rbuf[k, 64:80].astype(f32) for k in range(16)]
@@ -241,77 +252,118 @@
         axis=0,
     )
     a, b = iota((64, 256), 0), iota((64, 256), 1)
-    wanted = lax.rem(a, 16) * 8 + 2 * lax.div(a, 16) + lax.div(b, 128)
+    place = 2 * lax.div(a, 16) + lax.div(b, 128)
+    wanted = lax.rem(a, 16) * 8 + 2 * lax.rem(place, 4) + lax.div(place, 4)
     pick = jnp.where(lax.rem(b, 128) == wanted, 1.0, 0.0).astype(bf16)
     laid = dot(pick, stacked, NT).astype(bf16)
     for g in range(4):
-        zbuf[p, :, 128 * g : 128 * g + 128] = laid[16 * g : 16 * g + 16]
-
-    sends = []
-
-    def zsend(src, dst, o):
-        n = len(sends)
-        copy = remote(src, dst, zssem.at[n], zrsem.at[n], zoff(o), s)
-        copy.start()
-        sends.append(copy)
-        return copy
-
-    first = [zsend(zbuf.at[p], zbuf.at[p], o) for o in FAR]
-    second = [zsend(zbuf.at[p], zbuf.at[p], o) for o in NEAR]
-    for o, copy in zip(FAR, first):
-        copy.wait_recv()
-        q = zoff(-o)
-        if abs(o) == 6:
-            lanes = pl.ds(0 if o > 0 else 256, 256)
-            part_ref = zbuf.at[q, :, lanes]
-            second.append(zsend(part_ref, part_ref, 2 if o > 0 else -2))
-        for n in NEAR:
-            second.append(zsend(zbuf.at[q], zbuf.at[q], n))
-    for copy in second:
-        copy.wait_recv()
-
-    wait_bytes(wbuf, rsem.at[4])
-    terms = dot(zbuf[...].reshape(256, 512), wbuf[...].reshape(512, 512))
-    psend[...] = terms.astype(bf16).reshape(16, 16, 512)
-    mine = lax.rem(x, 2) * 8 + 2 * y + c
-    for dy, dx in HOPS:
-        prompt = lax.rem(y + dy, 4) * 4 + lax.rem(x + dx, 4)
-        send_or_keep(psend.at[prompt], obuf.at[mine], 7, 2 * prompt + lax.div(x, 2))
-    wait_bytes(obuf, rsem.at[7])
+        laid_ref[:, 128 * g : 128 * g + 128] = laid[16 * g : 16 * g + 16]
+
+    parity = lax.rem(p, 2)
+    own_slot = zbuf.at[lax.div(p, 2)]
+    for o in DIRECT:
+        remote(
+            laid_ref, own_slot.at[c], zssem.at[0], zrsem.at[lax.div(p, 2)], zoff(o), s - c + parity
+        ).start()
+
+    @pl.when(c == parity)
+    def _():
+        pltpu.make_async_copy(laid_ref, own_slot.at[c], zrsem.at[lax.div(p, 2)]).start()
+
+    @pl.when(c != parity)
+    def _():
+        remote(laid_ref, own_slot.at[c], zssem.at[1], zrsem.at[lax.div(p, 2)], p, sib).start()
+
+    wait_bytes(wbuf.at[c], rsem.at[4])
+    remote(wbuf.at[c], wbuf.at[c], ssem.at[7], rsem.at[8], p, sib).start()
+
+    def zwait(q):
+        wait_bytes(zbuf.at[lax.div(q, 2)], zrsem.at[lax.div(q, 2)])
+
+    def relay(source, onward):
+        for sign in (1, -1):
+            q = zoff(-sign * source)
+            zwait(q)
+            slot = lax.div(q, 2)
+            for o in onward:
+                remote(
+                    zbuf.at[slot], zbuf.at[slot], zssem.at[2], zrsem.at[slot], zoff(sign * o), s
+                ).start()
+
+    odd = lax.rem(p + c, 2)
+
+    @pl.when(odd == 1)
+    def _():
+        relay(5, (2, 1, -1))
+
+    @pl.when(odd == 0)
+    def _():
+        relay(2, (1,))
+
+    wait_bytes(wbuf.at[other], rsem.at[8])
+    mine = lax.rem(x, 2) * 4 + y
+    near = (5 * odd + 2 * (1 - odd), -5 * odd - 2 * (1 - odd), odd, 8 - 9 * odd)
+    far = (3 * odd + 4 * (1 - odd), -3 * odd - 4 * (1 - odd), 7 * odd + 6 * (1 - odd), -7 * odd - 6 * (1 - odd))
+    for n, group in enumerate((near, far)):
+        planes = [zoff(o) for o in group]
+        for q in planes[2:] if n == 0 else planes:
+            zwait(q)
+        terms = 0.0
+        for half in range(2):
+            rows = jnp.concatenate([zbuf[lax.div(q, 2), half] for q in planes], axis=0)
+            for core in range(2):
+                terms = terms + dot(
+                    rows[:, 256 * core : 256 * core + 256], wbuf[core, half].reshape(256, 512)
+                )
+        psend[4 * n : 4 * n + 4] = terms.astype(bf16).reshape(4, 16, 512)
+        for k, q in enumerate(planes):
+            send_or_keep(psend.at[4 * n + k], obuf.at[mine], 9, 2 * q + lax.div(x, 2))
+    wait_bytes(obuf, rsem.at[9])
     for half in range(2):
-        result = obuf[8 * half].astype(f32)
-        for k in range(1, 8):
-            result = result + obuf[8 * half + k].astype(f32)
+        result = obuf[4 * half].astype(f32)
+        for k in range(1, 4):
+            result = result + obuf[4 * half + k].astype(f32)
         out_ref[16 * half : 16 * half + 16, :] = result.astype(bf16)
 
     wait_bytes(qbuf.at[pl.ds(0, 31)], ssem.at[0])
     for copy in swap:
         copy.wait_send()
     tail_copy.wait_send()
-    for copy in sends:
-        copy.wait_send()
-    wait_bytes(wbuf.at[pl.ds(0, 7)], ssem.at[4])
+    wait_bytes(wbuf.at[0, :, pl.ds(0, 3)], ssem.at[4])
     wait_bytes(rbuf.at[pl.ds(0, 15)], ssem.at[6])
-    wait_bytes(obuf.at[pl.ds(0, 15)], ssem.at[7])
 
     @pl.when(lax.div(y, 2) != c)
     def _():
         wait_bytes(rbuf.at[15], ssem.at[6])
 
-    @pl.when(lax.div(x, 2) != c)
-    def _():
-        wait_bytes(obuf.at[15], ssem.at[7])
+    wait_bytes(wbuf.at[0], ssem.at[7])
+    wait_bytes(zbuf.at[pl.ds(0, len(DIRECT)), 0], zssem.at[0])
+
+    @pl.when(c != parity)
+    def _():
+        wait_bytes(laid_ref, zssem.at[1])
+
+    wait_bytes(zbuf.at[pl.ds(0, 2)], zssem.at[2])
+
+    @pl.when(odd == 1)
+    def _():
+        wait_bytes(zbuf.at[pl.ds(0, 4)], zssem.at[2])
+
+    wait_bytes(obuf.at[pl.ds(0, 7)], ssem.at[9])
+
+    @pl.when(x != 3 * c)
+    def _():
+        wait_bytes(obuf.at[7], ssem.at[9])
 
 
 def on_device(*args):
-    any_spec = pl.BlockSpec(memory_space=pl.ANY)
-    smem = pl.BlockSpec(memory_space=pltpu.SMEM)
-    specs = [any_spec] * 10
-    specs[3] = specs[6] = smem
+    args = list(args)
+    args[3] = jnp.transpose(args[3], (0, 2, 1))
+    args[9] = args[9].reshape(2, 64, 512)
     return pl.pallas_call(
         kernel,
         out_shape=jax.ShapeDtypeStruct((32, 512), bf16),
-        in_specs=specs,
+        in_specs=[pl.BlockSpec(memory_space=pltpu.HBM)] * 10,
         out_specs=pl.BlockSpec(memory_space=pltpu.VMEM),
         scratch_shapes=[
             pltpu.VMEM((2, 32, 128), bf16),
@@ -331,18 +383,21 @@
             pltpu.VMEM((2, 2, 136, 128), f32),
             pltpu.VMEM((4, 2, 2, 80, 128), bf16),
             pltpu.VMEM((16, 80, 128), bf16),
-            pltpu.VMEM((16, 16, 512), bf16),
-            pltpu.VMEM((8, 64, 512), bf16),
-            pltpu.VMEM((16, 16, 512), bf16),
-            pltpu.VMEM((16, 16, 512), bf16),
-            pltpu.SemaphoreType.DMA((7,)),
+            pltpu.VMEM((16, 512), bf16),
+            pltpu.VMEM((8, 2, 16, 512), bf16),
+            pltpu.VMEM((2, 2, 4, 64, 512), bf16),
+            pltpu.VMEM((8, 16, 512), bf16),
+            pltpu.VMEM((8, 16, 512), bf16),
+            pltpu.SMEM((1, 1, 4), jnp.int32),
+            pltpu.SMEM((1, 1), jnp.int32),
+            pltpu.SemaphoreType.DMA((9,)),
+            pltpu.SemaphoreType.DMA((10,)),
+            pltpu.SemaphoreType.DMA((10,)),
+            pltpu.SemaphoreType.DMA((3,)),
             pltpu.SemaphoreType.DMA((8,)),
-            pltpu.SemaphoreType.DMA((8,)),
-            pltpu.SemaphoreType.DMA((16,)),
-            pltpu.SemaphoreType.DMA((16,)),
         ],
         compiler_params=pltpu.CompilerParams(
-            collective_id=0, has_side_effects=True, vmem_limit_bytes=32 * 1024 * 1024
+            collective_id=0, has_side_effects=True, vmem_limit_bytes=56 * 1024 * 1024
         ),
         name="attend",
     )(*args)

time: 58.5 us -> 50.4 us (0.86)
  the two profiles are of different devices: /device:TPU:1 before, /device:TPU:25 now
where the time goes in v2:
time: 50.4 us; the launch traced here: 50.2 us
  Pallas kernels  48.2 us (96%)
  local copies, waits for them, and re-layouts  1.38 us (3%)
  between operations  0.66 us (1%)
    pallas_call x1, Pallas kernels, on_device(): pl.pallas_call(kernel, out_shape=jax.ShapeDtypeStruct((32, 512), bf16), i...  48.2 us
    unnamed x1, local copies, waits for them, and re-layouts  1.38 us

profile of v2, /device:TPU:25, one launch (start us, length us, event | category | flops | bytes accessed | tf_op | source)
XLA Modules:
  0.0 50.2 jit_solution(970204947002073929)
XLA Ops:
  0.7 48.2 %attend.1 = bf16[32,512]{1,0:T(8,128)(2,1)} custom-call(bf16[1,1,2,32,128]{4,3,2,1,0:T(8,128)(2,1)} %q_ref.1, bf16[1,4,256,128]{3,2,1,0:T(8,128)(2,1)} %k_ref.1, bf16[1,4,256,128]{3,2,1,0:T(8,128)(2,1)} %v_ref.1, s32[1,1,4]{2,1,0:T(1,128)} %bitcast.3, bf16[1,1,4,256,128]{4,3,2,1,0:T(8,128)(2,1)} %sk_ref.1, bf16[1,1,4,256,128]{4,3,2,1,0:T(8,128)(2,1)} %sv_ref.1, ...), custom_call_target="tpu_custom_call" | custom-call | tf_op jit(solution)/shard_map/attend/pallas_call | solution.py:363
  48.8 1.4 %copy.13 = bf16[32,512]{1,0:T(8,128)(2,1)} copy(bf16[32,512]{1,0:T(8,128)(2,1)} %attend.1) | data formatting | bytes 65536

commit v3 on v2

--- a/solution.py
+++ b/solution.py
@@ -35,10 +35,10 @@
 
 def kernel(
     q_ref, k_ref, v_ref, kept_hbm, sk_ref, sv_ref, len_hbm, dk_ref, dv_ref, w_ref,
-    out_ref,
+    obuf,
     qv, qsend, qbuf, kbuf, vbuf, vt, skv, svv, dkv, dvv, flag_out, flag, qpl,
-    tail_out, tail, part, rbuf, laid_ref, zbuf, wbuf, psend, obuf,
-    kept_ref, len_ref, lsem, ssem, rsem, zssem, zrsem,
+    tail_out, tail, part, rbuf, laid_ref, zbuf, wbuf, psend,
+    kept_ref, len_ref, lsem, ssem, rsem, zssem, zrsem, qrsem, known,
 ):
     p, s = lax.axis_index("prompt"), lax.axis_index("seq")
     y, i = lax.div(s, 8), lax.rem(s, 8)
@@ -94,7 +94,7 @@
         return carry
 
     lax.fori_loop(1, NS, greet, 0)
-    for o in DIRECT:
+    for o in (2, -2, 1, -1):
         for seq in (s, sib):
             pl.semaphore_signal(barrier, inc=1, device_id=at(zoff(o), seq), device_id_type=MESH)
 
@@ -113,30 +113,6 @@
     local[7].wait()
     flag[c] = flags(c)
     flag_out[...] = flags(other)
-
-    pl.semaphore_wait(barrier, NS - 1 + 2 * len(DIRECT))
-
-    for dy, dx in HOPS:
-        base = lax.rem(y + dy, 4) * 8 + lax.rem(x + dx, 4) * 2
-        for core in range(2):
-            if (dy, dx) != (0, 0):
-                remote(
-                    qsend.at[pl.ds(2 * core, 2)], qbuf.at[s], ssem.at[0], rsem.at[0], p, base + core
-                ).start()
-    remote(qsend.at[pl.ds(2 * other, 2)], qbuf.at[s], ssem.at[0], rsem.at[0], p, sib).start()
-    pltpu.make_async_copy(qsend.at[pl.ds(2 * c, 2)], qbuf.at[s], rsem.at[0]).start()
-    swap = [
-        remote(k_ref.at[0, pl.ds(2 * other, 2)], kbuf.at[c], ssem.at[1], rsem.at[1], p, sib),
-        remote(v_ref.at[0, pl.ds(2 * other, 2)], vbuf.at[c], ssem.at[2], rsem.at[2], p, sib),
-        remote(flag_out, flag.at[c], ssem.at[3], rsem.at[3], p, sib),
-    ]
-    for copy in swap:
-        copy.start()
-    for dx in (2, 1, 3):
-        remote(
-            w_ref, wbuf.at[c, :, x], ssem.at[4], rsem.at[4], p, y * 8 + lax.rem(x + dx, 4) * 2 + c
-        ).start()
-    pltpu.make_async_copy(w_ref, wbuf.at[c, :, x], rsem.at[4]).start()
 
     lane = iota((1, 128), 1)
     qpl[...] = jnp.zeros((4, 128, 128), bf16)
@@ -176,19 +152,47 @@
             tail_out[j, :128] = o
             tail_out[j, 128:] = stats
 
+    local[5].wait()
+    local[6].wait()
+    for j in range(2):
+        vt[j, c] = jnp.transpose(vbuf[c, j])
+
+    pl.semaphore_wait(barrier, NS - 1 + 8)
+
+    def spread(n, o):
+        for sign in (1, -1):
+            pl.semaphore_signal(
+                known.at[n], inc=1, device_id=at(zoff(sign * o), s), device_id_type=MESH
+            )
+
+    spread(0, 2)
+
+    swap = [
+        remote(k_ref.at[0, pl.ds(2 * other, 2)], kbuf.at[c], ssem.at[1], rsem.at[1], p, sib),
+        remote(v_ref.at[0, pl.ds(2 * other, 2)], vbuf.at[c], ssem.at[2], rsem.at[2], p, sib),
+        remote(flag_out, flag.at[c], ssem.at[3], rsem.at[3], p, sib),
+    ]
+    for copy in swap:
+        copy.start()
     tail_copy = remote(tail_out, tail.at[c], ssem.at[5], rsem.at[5], p, sib)
     tail_copy.start()
 
-    local[5].wait()
-    local[6].wait()
+
+    for dy, dx in reversed(HOPS):
+        base = lax.rem(y + dy, 4) * 8 + lax.rem(x + dx, 4) * 2
+        for core in range(2):
+            if (dy, dx) != (0, 0):
+                remote(
+                    qsend.at[pl.ds(2 * core, 2)], qbuf.at[s], ssem.at[0], qrsem.at[y], p, base + core
+                ).start()
+    remote(qsend.at[pl.ds(2 * other, 2)], qbuf.at[s], ssem.at[0], qrsem.at[y], p, sib).start()
+    pltpu.make_async_copy(qsend.at[pl.ds(2 * c, 2)], qbuf.at[s], qrsem.at[y]).start()
     for n in (1, 2, 3):
         swap[n - 1].wait_recv()
     for j in range(2):
-        for core in range(2):
-            vt[j, core] = jnp.transpose(vbuf[core, j])
+        vt[j, other] = jnp.transpose(vbuf[other, j])
     tail_copy.wait_recv()
 
-    wait_bytes(qbuf, rsem.at[0])
     def partial(kk, j):
         chunk = lax.rem(y + kk, 4)
         rows = qbuf[pl.ds(8 * chunk, 8), j].reshape(128, 128)
@@ -225,19 +229,27 @@
             part[kk, j, half, :64] = summed[64 * half : 64 * half + 64]
             part[kk, j, half, 64:] = stats
 
-    for group in ((0, 1), (2, 3)):
-        for kk in group:
-            for j in range(2):
-                partial(kk, j)
-        for kk in group:
-            chunk = lax.rem(y + kk, 4)
-            for j in range(2):
-                for half in range(2):
-                    send_or_keep(
-                        part.at[kk, j, half], rbuf.at[chip], 6, (2 * c + j) * 8 + chunk * 2 + half
-                    )
+    for kk in (0, 1, 3, 2):
+        chunk = lax.rem(y + kk, 4)
+        wait_bytes(qbuf.at[pl.ds(8 * chunk, 8)], qrsem.at[chunk])
+        for j in range(2):
+            partial(kk, j)
+        for j in range(2):
+            for half in range(2):
+                send_or_keep(
+                    part.at[kk, j, half], rbuf.at[chip], 6, (2 * c + j) * 8 + chunk * 2 + half
+                )
+
+    pl.semaphore_wait(known.at[0], 2)
+    spread(1, 4)
 
     wait_bytes(rbuf, rsem.at[6])
+    for dx in (2, 1, 3):
+        remote(
+            w_ref, wbuf.at[c, :, x], ssem.at[4], rsem.at[4], p, y * 8 + lax.rem(x + dx, 4) * 2 + c
+        ).start()
+    pltpu.make_async_copy(w_ref, wbuf.at[c, :, x], rsem.at[4]).start()
+
     tops = [rbuf[k, 64:80].astype(f32) for k in range(16)]
     top = functools.reduce(jnp.maximum, [t[0:1] for t in tops])
     total, summed = 0.0, 0.0
@@ -259,6 +271,7 @@
     for g in range(4):
         laid_ref[:, 128 * g : 128 * g + 128] = laid[16 * g : 16 * g + 16]
 
+    pl.semaphore_wait(known.at[1], 2)
     parity = lax.rem(p, 2)
     own_slot = zbuf.at[lax.div(p, 2)]
     for o in DIRECT:
@@ -273,9 +286,6 @@
     @pl.when(c != parity)
     def _():
         remote(laid_ref, own_slot.at[c], zssem.at[1], zrsem.at[lax.div(p, 2)], p, sib).start()
-
-    wait_bytes(wbuf.at[c], rsem.at[4])
-    remote(wbuf.at[c], wbuf.at[c], ssem.at[7], rsem.at[8], p, sib).start()
 
     def zwait(q):
         wait_bytes(zbuf.at[lax.div(q, 2)], zrsem.at[lax.div(q, 2)])
@@ -299,6 +309,9 @@
     @pl.when(odd == 0)
     def _():
         relay(2, (1,))
+
+    wait_bytes(wbuf.at[c], rsem.at[4])
+    remote(wbuf.at[c], wbuf.at[c], ssem.at[7], rsem.at[8], p, sib).start()
 
     wait_bytes(wbuf.at[other], rsem.at[8])
     mine = lax.rem(x, 2) * 4 + y
@@ -319,12 +332,6 @@
         for k, q in enumerate(planes):
             send_or_keep(psend.at[4 * n + k], obuf.at[mine], 9, 2 * q + lax.div(x, 2))
     wait_bytes(obuf, rsem.at[9])
-    for half in range(2):
-        result = obuf[4 * half].astype(f32)
-        for k in range(1, 4):
-            result = result + obuf[4 * half + k].astype(f32)
-        out_ref[16 * half : 16 * half + 16, :] = result.astype(bf16)
-
     wait_bytes(qbuf.at[pl.ds(0, 31)], ssem.at[0])
     for copy in swap:
         copy.wait_send()
@@ -360,11 +367,11 @@
     args = list(args)
     args[3] = jnp.transpose(args[3], (0, 2, 1))
     args[9] = args[9].reshape(2, 64, 512)
-    return pl.pallas_call(
+    terms = pl.pallas_call(
         kernel,
-        out_shape=jax.ShapeDtypeStruct((32, 512), bf16),
+        out_shape=jax.ShapeDtypeStruct((8, 16, 512), bf16),
         in_specs=[pl.BlockSpec(memory_space=pltpu.HBM)] * 10,
-        out_specs=pl.BlockSpec(memory_space=pltpu.VMEM),
+        out_specs=pl.BlockSpec(memory_space=pltpu.HBM),
         scratch_shapes=[
             pltpu.VMEM((2, 32, 128), bf16),
             pltpu.VMEM((4, 16, 128), bf16),
@@ -387,7 +394,6 @@
             pltpu.VMEM((8, 2, 16, 512), bf16),
             pltpu.VMEM((2, 2, 4, 64, 512), bf16),
             pltpu.VMEM((8, 16, 512), bf16),
-            pltpu.VMEM((8, 16, 512), bf16),
             pltpu.SMEM((1, 1, 4), jnp.int32),
             pltpu.SMEM((1, 1), jnp.int32),
             pltpu.SemaphoreType.DMA((9,)),
@@ -395,12 +401,16 @@
             pltpu.SemaphoreType.DMA((10,)),
             pltpu.SemaphoreType.DMA((3,)),
             pltpu.SemaphoreType.DMA((8,)),
+            pltpu.SemaphoreType.DMA((4,)),
+            pltpu.SemaphoreType.REGULAR((2,)),
         ],
         compiler_params=pltpu.CompilerParams(
             collective_id=0, has_side_effects=True, vmem_limit_bytes=56 * 1024 * 1024
         ),
         name="attend",
     )(*args)
+    terms = terms.reshape(2, 4, 16, 512).astype(f32)
+    return jnp.sum(terms, axis=1).reshape(32, 512).astype(bf16)
 
 
 def solution(mesh):

time: 50.4 us -> 47.2 us (0.937)
  the two profiles are of different devices: /device:TPU:25 before, /device:TPU:24 now
where the time goes in v3:
time: 47.2 us; the launch traced here: 47.1 us
  Pallas kernels  44.8 us (95%)
  other arithmetic  1.55 us (3%)
  between operations  0.66 us (1%)
    pallas_call x1, Pallas kernels, on_device(): pl.pallas_call(kernel, out_shape=jax.ShapeDtypeStruct((8, 16, 512), bf16)...  44.8 us
    reduce_sum x1, other arithmetic, on_device(): return jnp.sum(terms, axis=1).reshape(32, 512).astype(bf16)  1.55 us

profile of v3, /device:TPU:24, one launch (start us, length us, event | category | flops | bytes accessed | tf_op | source)
XLA Modules:
  0.0 47.1 jit_solution(16131214421125470288)
XLA Ops:
  0.7 44.8 %attend.1 = bf16[8,16,512]{2,1,0:T(8,128)(2,1)} custom-call(bf16[1,1,2,32,128]{4,3,2,1,0:T(8,128)(2,1)} %q_ref.1, bf16[1,4,256,128]{3,2,1,0:T(8,128)(2,1)} %k_ref.1, bf16[1,4,256,128]{3,2,1,0:T(8,128)(2,1)} %v_ref.1, s32[1,1,4]{2,1,0:T(1,128)} %bitcast.6, bf16[1,1,4,256,128]{4,3,2,1,0:T(8,128)(2,1)} %sk_ref.1, bf16[1,1,4,256,128]{4,3,2,1,0:T(8,128)(2,1)} %sv_ref.1, ...), custom_call_target="tpu_custom_call" | custom-call | tf_op jit(solution)/shard_map/attend/pallas_call | solution.py:370
  45.5 1.6 %bitcast_reduce_fusion = bf16[2,16,512]{2,1,0:T(8,128)(2,1)} fusion(bf16[8,16,512]{2,1,0:T(8,128)(2,1)} %attend.1), kind=kLoop, calls=%fused_computation | loop fusion | flops 49152 | bytes 163840 | tf_op jit(solution)/shard_map/reduce_sum | solution.py:413

commit v4 on v3

--- a/solution.py
+++ b/solution.py
@@ -16,7 +16,7 @@
 NP = 16
 NS = 32
 SCALE = 1.0 / math.sqrt(128)
-DIRECT = (8, 5, -5, 2, -2, 1, -1)
+DIRECT = (5, -5, 8, 2, -2, 1, -1)
 HOPS = sorted(
     ((dy, dx) for dy in range(4) for dx in range(4)),
     key=lambda t: -(min(t[0], 4 - t[0]) + min(t[1], 4 - t[1])),

time: 47.2 us -> 46.4 us (0.983)
  the two profiles are of different devices: /device:TPU:24 before, /device:TPU:1 now
where the time goes in v4:
time: 46.4 us; the launch traced here: 46.2 us
  Pallas kernels  44 us (95%)
  other arithmetic  1.55 us (3%)
  between operations  0.66 us (1%)
    pallas_call x1, Pallas kernels, on_device(): pl.pallas_call(kernel, out_shape=jax.ShapeDtypeStruct((8, 16, 512), bf16)...  44 us
    reduce_sum x1, other arithmetic, on_device(): return jnp.sum(terms, axis=1).reshape(32, 512).astype(bf16)  1.55 us

profile of v4, /device:TPU:1, one launch (start us, length us, event | category | flops | bytes accessed | tf_op | source)
XLA Modules:
  0.0 46.2 jit_solution(16961921789127553605)
XLA Ops:
  0.7 44.0 %attend.1 = bf16[8,16,512]{2,1,0:T(8,128)(2,1)} custom-call(bf16[1,1,2,32,128]{4,3,2,1,0:T(8,128)(2,1)} %q_ref.1, bf16[1,4,256,128]{3,2,1,0:T(8,128)(2,1)} %k_ref.1, bf16[1,4,256,128]{3,2,1,0:T(8,128)(2,1)} %v_ref.1, s32[1,1,4]{2,1,0:T(1,128)} %bitcast.6, bf16[1,1,4,256,128]{4,3,2,1,0:T(8,128)(2,1)} %sk_ref.1, bf16[1,1,4,256,128]{4,3,2,1,0:T(8,128)(2,1)} %sv_ref.1, ...), custom_call_target="tpu_custom_call" | custom-call | tf_op jit(solution)/shard_map/attend/pallas_call | solution.py:370
  44.7 1.6 %bitcast_reduce_fusion = bf16[2,16,512]{2,1,0:T(8,128)(2,1)} fusion(bf16[8,16,512]{2,1,0:T(8,128)(2,1)} %attend.1), kind=kLoop, calls=%fused_computation | loop fusion | flops 49152 | bytes 163840 | tf_op jit(solution)/shard_map/reduce_sum | solution.py:413

commit v5 on v4

--- a/solution.py
+++ b/solution.py
@@ -246,9 +246,11 @@
     wait_bytes(rbuf, rsem.at[6])
     for dx in (2, 1, 3):
         remote(
-            w_ref, wbuf.at[c, :, x], ssem.at[4], rsem.at[4], p, y * 8 + lax.rem(x + dx, 4) * 2 + c
+            w_ref, wbuf.at[c, :, x], ssem.at[4], rsem.at[8 if dx == 2 else 4], p,
+            y * 8 + lax.rem(x + dx, 4) * 2 + c,
         ).start()
-    pltpu.make_async_copy(w_ref, wbuf.at[c, :, x], rsem.at[4]).start()
+    pltpu.make_async_copy(w_ref, wbuf.at[c, :, x], lsem.at[9]).start()
+    remote(w_ref, wbuf.at[c, :, x], ssem.at[7], rsem.at[7], p, sib).start()
 
     tops = [rbuf[k, 64:80].astype(f32) for k in range(16)]
     top = functools.reduce(jnp.maximum, [t[0:1] for t in tops])
@@ -310,14 +312,24 @@
     def _():
         relay(2, (1,))
 
-    wait_bytes(wbuf.at[c], rsem.at[4])
-    remote(wbuf.at[c], wbuf.at[c], ssem.at[7], rsem.at[8], p, sib).start()
-
-    wait_bytes(wbuf.at[other], rsem.at[8])
+    def forward(dx):
+        block = wbuf.at[c, :, lax.rem(x + dx, 4)]
+        remote(block, block, ssem.at[7], rsem.at[7], p, sib).start()
+
+    wait_bytes(wbuf.at[c, :, pl.ds(0, 2)], rsem.at[4])
+    forward(1)
+    forward(3)
+    wait_bytes(wbuf.at[c, :, 0], rsem.at[8])
+    forward(2)
+    wait_bytes(wbuf.at[c, :, 0], lsem.at[9])
+
+    wait_bytes(wbuf.at[other], rsem.at[7])
     mine = lax.rem(x, 2) * 4 + y
     near = (5 * odd + 2 * (1 - odd), -5 * odd - 2 * (1 - odd), odd, 8 - 9 * odd)
-    far = (3 * odd + 4 * (1 - odd), -3 * odd - 4 * (1 - odd), 7 * odd + 6 * (1 - odd), -7 * odd - 6 * (1 - odd))
-    for n, group in enumerate((near, far)):
+    middle = (3 * odd + 4 * (1 - odd), -3 * odd - 4 * (1 - odd))
+    far = (7 * odd + 6 * (1 - odd), -7 * odd - 6 * (1 - odd))
+    done = 0
+    for n, group in enumerate((near, middle, far)):
         planes = [zoff(o) for o in group]
         for q in planes[2:] if n == 0 else planes:
             zwait(q)
@@ -328,9 +340,10 @@
                 terms = terms + dot(
                     rows[:, 256 * core : 256 * core + 256], wbuf[core, half].reshape(256, 512)
                 )
-        psend[4 * n : 4 * n + 4] = terms.astype(bf16).reshape(4, 16, 512)
+        psend[done : done + len(group)] = terms.astype(bf16).reshape(len(group), 16, 512)
         for k, q in enumerate(planes):
-            send_or_keep(psend.at[4 * n + k], obuf.at[mine], 9, 2 * q + lax.div(x, 2))
+            send_or_keep(psend.at[done + k], obuf.at[mine], 9, 2 * q + lax.div(x, 2))
+        done += len(group)
     wait_bytes(obuf, rsem.at[9])
     wait_bytes(qbuf.at[pl.ds(0, 31)], ssem.at[0])
     for copy in swap:
@@ -396,7 +409,7 @@
             pltpu.VMEM((8, 16, 512), bf16),
             pltpu.SMEM((1, 1, 4), jnp.int32),
             pltpu.SMEM((1, 1), jnp.int32),
-            pltpu.SemaphoreType.DMA((9,)),
+            pltpu.SemaphoreType.DMA((10,)),
             pltpu.SemaphoreType.DMA((10,)),
             pltpu.SemaphoreType.DMA((10,)),
             pltpu.SemaphoreType.DMA((3,)),

time: 46.4 us -> 46.4 us (level)
  no operation moved by 1% of the time
where the time goes in v5:
time: 46.4 us; the launch traced here: 46.2 us
  Pallas kernels  44 us (95%)
  other arithmetic  1.55 us (3%)
  between operations  0.66 us (1%)
    pallas_call x1, Pallas kernels, on_device(): pl.pallas_call(kernel, out_shape=jax.ShapeDtypeStruct((8, 16, 512), bf16)...  44 us
    reduce_sum x1, other arithmetic, on_device(): return jnp.sum(terms, axis=1).reshape(32, 512).astype(bf16)  1.55 us

profile of v5, /device:TPU:1, one launch (start us, length us, event | category | flops | bytes accessed | tf_op | source)
XLA Modules:
  0.0 46.2 jit_solution(17968647843442296868)
XLA Ops:
  0.7 44.0 %attend.1 = bf16[8,16,512]{2,1,0:T(8,128)(2,1)} custom-call(bf16[1,1,2,32,128]{4,3,2,1,0:T(8,128)(2,1)} %q_ref.1, bf16[1,4,256,128]{3,2,1,0:T(8,128)(2,1)} %k_ref.1, bf16[1,4,256,128]{3,2,1,0:T(8,128)(2,1)} %v_ref.1, s32[1,1,4]{2,1,0:T(1,128)} %bitcast.6, bf16[1,1,4,256,128]{4,3,2,1,0:T(8,128)(2,1)} %sk_ref.1, bf16[1,1,4,256,128]{4,3,2,1,0:T(8,128)(2,1)} %sv_ref.1, ...), custom_call_target="tpu_custom_call" | custom-call | tf_op jit(solution)/shard_map/attend/pallas_call | solution.py:383
  44.7 1.6 %bitcast_reduce_fusion = bf16[2,16,512]{2,1,0:T(8,128)(2,1)} fusion(bf16[8,16,512]{2,1,0:T(8,128)(2,1)} %attend.1), kind=kLoop, calls=%fused_computation | loop fusion | flops 49152 | bytes 163840 | tf_op jit(solution)/shard_map/reduce_sum | solution.py:426

commit v6 on v4

--- a/solution.py
+++ b/solution.py
@@ -291,11 +291,14 @@
         wait_bytes(zbuf.at[lax.div(q, 2)], zrsem.at[lax.div(q, 2)])
 
     def relay(source, onward):
-        for sign in (1, -1):
-            q = zoff(-sign * source)
-            zwait(q)
-            slot = lax.div(q, 2)
-            for o in onward:
+        slots = []
+        for k, o in enumerate(onward):
+            for n, sign in enumerate((1, -1)):
+                if k == 0:
+                    q = zoff(-sign * source)
+                    zwait(q)
+                    slots.append(lax.div(q, 2))
+                slot = slots[n]
                 remote(
                     zbuf.at[slot], zbuf.at[slot], zssem.at[2], zrsem.at[slot], zoff(sign * o), s
                 ).start()

time: 46.4 us -> 46.4 us (level)
  no operation moved by 1% of the time
where the time goes in v6:
time: 46.4 us; the launch traced here: 46.2 us
  Pallas kernels  44 us (95%)
  other arithmetic  1.55 us (3%)
  between operations  0.66 us (1%)
    pallas_call x1, Pallas kernels, on_device(): pl.pallas_call(kernel, out_shape=jax.ShapeDtypeStruct((8, 16, 512), bf16)...  44 us
    reduce_sum x1, other arithmetic, on_device(): return jnp.sum(terms, axis=1).reshape(32, 512).astype(bf16)  1.55 us

profile of v6, /device:TPU:1, one launch (start us, length us, event | category | flops | bytes accessed | tf_op | source)
XLA Modules:
  0.0 46.2 jit_solution(2741593439832724220)
XLA Ops:
  0.7 44.0 %attend.1 = bf16[8,16,512]{2,1,0:T(8,128)(2,1)} custom-call(bf16[1,1,2,32,128]{4,3,2,1,0:T(8,128)(2,1)} %q_ref.1, bf16[1,4,256,128]{3,2,1,0:T(8,128)(2,1)} %k_ref.1, bf16[1,4,256,128]{3,2,1,0:T(8,128)(2,1)} %v_ref.1, s32[1,1,4]{2,1,0:T(1,128)} %bitcast.6, bf16[1,1,4,256,128]{4,3,2,1,0:T(8,128)(2,1)} %sk_ref.1, bf16[1,1,4,256,128]{4,3,2,1,0:T(8,128)(2,1)} %sv_ref.1, ...), custom_call_target="tpu_custom_call" | custom-call | tf_op jit(solution)/shard_map/attend/pallas_call | solution.py:373
  44.7 1.6 %bitcast_reduce_fusion = bf16[2,16,512]{2,1,0:T(8,128)(2,1)} fusion(bf16[8,16,512]{2,1,0:T(8,128)(2,1)} %attend.1), kind=kLoop, calls=%fused_computation | loop fusion | flops 49152 | bytes 163840 | tf_op jit(solution)/shard_map/reduce_sum | solution.py:416

commit v7 on v4

--- a/solution.py
+++ b/solution.py
@@ -38,7 +38,7 @@
     obuf,
     qv, qsend, qbuf, kbuf, vbuf, vt, skv, svv, dkv, dvv, flag_out, flag, qpl,
     tail_out, tail, part, rbuf, laid_ref, zbuf, wbuf, psend,
-    kept_ref, len_ref, lsem, ssem, rsem, zssem, zrsem, qrsem, known,
+    kept_ref, len_ref, lsem, ssem, rsem, zssem, zrsem, qrsem, prsem, known,
 ):
     p, s = lax.axis_index("prompt"), lax.axis_index("seq")
     y, i = lax.div(s, 8), lax.rem(s, 8)
@@ -60,16 +60,17 @@
     def wait_bytes(ref, sem):
         pltpu.make_async_copy(ref, ref, sem).wait()
 
-    def send_or_keep(src, dst, n, seq):
+    def send_or_keep(src, dst, n, seq, recv=None):
+        recv = rsem.at[n] if recv is None else recv
         own = seq == s
 
         @pl.when(own)
         def _():
-            pltpu.make_async_copy(src, dst, rsem.at[n]).start()
+            pltpu.make_async_copy(src, dst, recv).start()
 
         @pl.when(jnp.logical_not(own))
         def _():
-            remote(src, dst, ssem.at[n], rsem.at[n], p, seq).start()
+            remote(src, dst, ssem.at[n], recv, p, seq).start()
 
     local = [
         pltpu.make_async_copy(q_ref.at[0, 0], qv, lsem.at[0]),
@@ -237,26 +238,39 @@
         for j in range(2):
             for half in range(2):
                 send_or_keep(
-                    part.at[kk, j, half], rbuf.at[chip], 6, (2 * c + j) * 8 + chunk * 2 + half
+                    part.at[kk, j, half], rbuf.at[chip], 6, (2 * c + j) * 8 + chunk * 2 + half,
+                    prsem.at[y],
                 )
 
     pl.semaphore_wait(known.at[0], 2)
     spread(1, 4)
 
-    wait_bytes(rbuf, rsem.at[6])
+    tops, sums, outs = [], [], []
+    for dy in (0, 1, 3, 2):
+        row = lax.rem(x - dy + 4, 4)
+        wait_bytes(rbuf.at[pl.ds(4 * row, 4)], prsem.at[row])
+        heads4 = [rbuf[4 * row + k, 64:80].astype(f32) for k in range(4)]
+        top = functools.reduce(jnp.maximum, [t[0:1] for t in heads4])
+        total, summed = 0.0, 0.0
+        for k in range(4):
+            factor = jnp.exp(heads4[k][0:1] - top)
+            total = total + factor * (heads4[k][1:2] + heads4[k][2:3])
+            summed = summed + factor * rbuf[4 * row + k, :64].astype(f32)
+        tops.append(top)
+        sums.append(total)
+        outs.append(summed)
     for dx in (2, 1, 3):
         remote(
             w_ref, wbuf.at[c, :, x], ssem.at[4], rsem.at[4], p, y * 8 + lax.rem(x + dx, 4) * 2 + c
         ).start()
     pltpu.make_async_copy(w_ref, wbuf.at[c, :, x], rsem.at[4]).start()
 
-    tops = [rbuf[k, 64:80].astype(f32) for k in range(16)]
-    top = functools.reduce(jnp.maximum, [t[0:1] for t in tops])
+    top = functools.reduce(jnp.maximum, tops)
     total, summed = 0.0, 0.0
-    for k in range(16):
-        factor = jnp.exp(tops[k][0:1] - top)
-        total = total + factor * (tops[k][1:2] + tops[k][2:3])
-        summed = summed + factor * rbuf[k, :64].astype(f32)
+    for m, part_sum, o in zip(tops, sums, outs):
+        factor = jnp.exp(m - top)
+        total = total + factor * part_sum
+        summed = summed + factor * o
     head_out = (summed / total).astype(bf16)
     blank = jnp.zeros_like(head_out)
     stacked = jnp.concatenate(
@@ -402,6 +416,7 @@
             pltpu.SemaphoreType.DMA((3,)),
             pltpu.SemaphoreType.DMA((8,)),
             pltpu.SemaphoreType.DMA((4,)),
+            pltpu.SemaphoreType.DMA((4,)),
             pltpu.SemaphoreType.REGULAR((2,)),
         ],
         compiler_params=pltpu.CompilerParams(

time: 46.4 us -> 46.5 us (level)
  no operation moved by 1% of the time
where the time goes in v7:
time: 46.5 us; the launch traced here: 46.3 us
  Pallas kernels  44.1 us (95%)
  other arithmetic  1.55 us (3%)
  between operations  0.66 us (1%)
    pallas_call x1, Pallas kernels, on_device(): pl.pallas_call(kernel, out_shape=jax.ShapeDtypeStruct((8, 16, 512), bf16)...  44.1 us
    reduce_sum x1, other arithmetic, on_device(): return jnp.sum(terms, axis=1).reshape(32, 512).astype(bf16)  1.55 us

profile of v7, /device:TPU:1, one launch (start us, length us, event | category | flops | bytes accessed | tf_op | source)
XLA Modules:
  0.0 46.3 jit_solution(15409895825278522383)
XLA Ops:
  0.7 44.1 %attend.1 = bf16[8,16,512]{2,1,0:T(8,128)(2,1)} custom-call(bf16[1,1,2,32,128]{4,3,2,1,0:T(8,128)(2,1)} %q_ref.1, bf16[1,4,256,128]{3,2,1,0:T(8,128)(2,1)} %k_ref.1, bf16[1,4,256,128]{3,2,1,0:T(8,128)(2,1)} %v_ref.1, s32[1,1,4]{2,1,0:T(1,128)} %bitcast.6, bf16[1,1,4,256,128]{4,3,2,1,0:T(8,128)(2,1)} %sk_ref.1, bf16[1,1,4,256,128]{4,3,2,1,0:T(8,128)(2,1)} %sv_ref.1, ...), custom_call_target="tpu_custom_call" | custom-call | tf_op jit(solution)/shard_map/attend/pallas_call | solution.py:384
  44.8 1.6 %bitcast_reduce_fusion = bf16[2,16,512]{2,1,0:T(8,128)(2,1)} fusion(bf16[8,16,512]{2,1,0:T(8,128)(2,1)} %attend.1), kind=kLoop, calls=%fused_computation | loop fusion | flops 49152 | bytes 163840 | tf_op jit(solution)/shard_map/reduce_sum | solution.py:428

commit v8 on v7

--- a/solution.py
+++ b/solution.py
@@ -261,9 +261,11 @@
         outs.append(summed)
     for dx in (2, 1, 3):
         remote(
-            w_ref, wbuf.at[c, :, x], ssem.at[4], rsem.at[4], p, y * 8 + lax.rem(x + dx, 4) * 2 + c
+            w_ref, wbuf.at[c, :, x], ssem.at[4], rsem.at[8 if dx == 2 else 4], p,
+            y * 8 + lax.rem(x + dx, 4) * 2 + c,
         ).start()
-    pltpu.make_async_copy(w_ref, wbuf.at[c, :, x], rsem.at[4]).start()
+    pltpu.make_async_copy(w_ref, wbuf.at[c, :, x], lsem.at[9]).start()
+    remote(w_ref, wbuf.at[c, :, x], ssem.at[7], rsem.at[7], p, sib).start()
 
     top = functools.reduce(jnp.maximum, tops)
     total, summed = 0.0, 0.0
@@ -305,11 +307,14 @@
         wait_bytes(zbuf.at[lax.div(q, 2)], zrsem.at[lax.div(q, 2)])
 
     def relay(source, onward):
-        for sign in (1, -1):
-            q = zoff(-sign * source)
-            zwait(q)
-            slot = lax.div(q, 2)
-            for o in onward:
+        slots = []
+        for k, o in enumerate(onward):
+            for n, sign in enumerate((1, -1)):
+                if k == 0:
+                    q = zoff(-sign * source)
+                    zwait(q)
+                    slots.append(lax.div(q, 2))
+                slot = slots[n]
                 remote(
                     zbuf.at[slot], zbuf.at[slot], zssem.at[2], zrsem.at[slot], zoff(sign * o), s
                 ).start()
@@ -324,10 +329,18 @@
     def _():
         relay(2, (1,))
 
-    wait_bytes(wbuf.at[c], rsem.at[4])
-    remote(wbuf.at[c], wbuf.at[c], ssem.at[7], rsem.at[8], p, sib).start()
-
-    wait_bytes(wbuf.at[other], rsem.at[8])
+    def forward(dx):
+        block = wbuf.at[c, :, lax.rem(x + dx, 4)]
+        remote(block, block, ssem.at[7], rsem.at[7], p, sib).start()
+
+    wait_bytes(wbuf.at[c, :, pl.ds(0, 2)], rsem.at[4])
+    forward(1)
+    forward(3)
+    wait_bytes(wbuf.at[c, :, 0], rsem.at[8])
+    forward(2)
+    wait_bytes(wbuf.at[c, :, 0], lsem.at[9])
+
+    wait_bytes(wbuf.at[other], rsem.at[7])
     mine = lax.rem(x, 2) * 4 + y
     near = (5 * odd + 2 * (1 - odd), -5 * odd - 2 * (1 - odd), odd, 8 - 9 * odd)
     far = (3 * odd + 4 * (1 - odd), -3 * odd - 4 * (1 - odd), 7 * odd + 6 * (1 - odd), -7 * odd - 6 * (1 - odd))
@@ -410,7 +423,7 @@
             pltpu.VMEM((8, 16, 512), bf16),
             pltpu.SMEM((1, 1, 4), jnp.int32),
             pltpu.SMEM((1, 1), jnp.int32),
-            pltpu.SemaphoreType.DMA((9,)),
+            pltpu.SemaphoreType.DMA((10,)),
             pltpu.SemaphoreType.DMA((10,)),
             pltpu.SemaphoreType.DMA((10,)),
             pltpu.SemaphoreType.DMA((3,)),

time: 46.5 us -> 46.4 us (level)
  no operation moved by 1% of the time
where the time goes in v8:
time: 46.4 us; the launch traced here: 46.2 us
  Pallas kernels  44 us (95%)
  other arithmetic  1.55 us (3%)
  between operations  0.66 us (1%)
    pallas_call x1, Pallas kernels, on_device(): pl.pallas_call(kernel, out_shape=jax.ShapeDtypeStruct((8, 16, 512), bf16)...  44 us
    reduce_sum x1, other arithmetic, on_device(): return jnp.sum(terms, axis=1).reshape(32, 512).astype(bf16)  1.55 us

profile of v8, /device:TPU:1, one launch (start us, length us, event | category | flops | bytes accessed | tf_op | source)
XLA Modules:
  0.0 46.2 jit_solution(609083176674931827)
XLA Ops:
  0.7 44.0 %attend.1 = bf16[8,16,512]{2,1,0:T(8,128)(2,1)} custom-call(bf16[1,1,2,32,128]{4,3,2,1,0:T(8,128)(2,1)} %q_ref.1, bf16[1,4,256,128]{3,2,1,0:T(8,128)(2,1)} %k_ref.1, bf16[1,4,256,128]{3,2,1,0:T(8,128)(2,1)} %v_ref.1, s32[1,1,4]{2,1,0:T(1,128)} %bitcast.6, bf16[1,1,4,256,128]{4,3,2,1,0:T(8,128)(2,1)} %sk_ref.1, bf16[1,1,4,256,128]{4,3,2,1,0:T(8,128)(2,1)} %sv_ref.1, ...), custom_call_target="tpu_custom_call" | custom-call | tf_op jit(solution)/shard_map/attend/pallas_call | solution.py:397
  44.7 1.6 %bitcast_reduce_fusion = bf16[2,16,512]{2,1,0:T(8,128)(2,1)} fusion(bf16[8,16,512]{2,1,0:T(8,128)(2,1)} %attend.1), kind=kLoop, calls=%fused_computation | loop fusion | flops 49152 | bytes 163840 | tf_op jit(solution)/shard_map/reduce_sum | solution.py:441
